TPU v7x, 256 devices: a whole 4x4x8 slice. The times are simulated.
256 devices in a mesh: tok: 2 (over x_hi), out: 16 (over x_lo, y, core), inp: 8 (over z).
Axes of the slice: x: 4 (x_hi: 2, x_lo: 2; x = x_hi * 2 + x_lo), y: 4, z: 8, core: 2. Of those that a mesh axis runs over, the one named last changes fastest.
Arguments:
- cand_grad: bfloat16 [256, 28672], P(None, ('tok', 'inp'))
- cand_act: bfloat16 [256, 8192], P(None, ('tok', 'out'))
- query_grad: bfloat16 [64, 28672], P(None, ('tok', 'inp'))
- query_act: bfloat16 [64, 8192], P(None, ('tok', 'out'))
- eig_out: bfloat16 [28672, 28672], P(('tok', 'inp'), 'out'), may hold values from -0.03125 to 0.03125
- eig_in: bfloat16 [8192, 8192], P(('tok', 'out'), 'inp'), may hold values from -0.0625 to 0.0625
- eigenvalues: bfloat16 [28672, 8192], P('out', 'inp'), as said below
- doc_lengths: int32 [16], replicated, may hold values from 1 to 64, 256 in all
- query_ids: int32 [64], replicated, may hold values from 0 to 3, never falling along the last dimension, each value on 1 to 32 neighbouring positions
Outputs:
- scores: float32 [16, 4], replicated
Inputs may be any that keep to these rules, and one draw needn't show every extreme that they name: `doc_lengths`: the lengths of the 16 documents sum to 256; the longest has exactly 64 tokens. `query_ids`: never falling; every query has one or more tokens, the longest exactly 32. `eigenvalues`: Positive.
All inputs are finite; a program needn't handle non-finite values.
Results may differ from a plain program's by a relative error of at most 0.0064.
Values may be sent and summed in bfloat16 or wider, within the bound.
A program may use at most 64 MiB of HBM per device.

v0:
```python
import jax
import jax.numpy as jnp
from jax import lax
from jax.sharding import PartitionSpec as P

D = 8192
FF = 28672
Q = 4


def local(
    cand_grad, cand_act, query_grad, query_act, eig_out, eig_in, eigenvalues, doc_lengths, query_ids
):
    tok_count = lax.axis_size("tok")
    cand_rows = cand_grad.shape[0]
    own_rows = cand_rows // tok_count
    own_start = lax.axis_index("tok") * own_rows
    values = eigenvalues.astype(jnp.float32)
    eigen_sum = lax.psum(jnp.sum(values), ("out", "inp"))
    damping = 0.1 * eigen_sum / (FF * D)
    inverse = 1.0 / (values + damping)
    cand_gsum, query_gsum = lax.psum(
        (
            jnp.dot(cand_grad, eig_out, preferred_element_type=jnp.float32),
            jnp.dot(query_grad, eig_out, preferred_element_type=jnp.float32),
        ),
        ("tok", "inp"),
    )
    query_grads = query_gsum.astype(jnp.bfloat16)
    cand_asum, query_asum = lax.psum(
        (
            jnp.dot(cand_act, eig_in, preferred_element_type=jnp.float32),
            jnp.dot(query_act, eig_in, preferred_element_type=jnp.float32),
        ),
        ("tok", "out"),
    )
    query_acts = query_asum.astype(jnp.bfloat16)
    score_grads = lax.dynamic_slice_in_dim(cand_gsum, own_start, own_rows, 0).astype(jnp.bfloat16)
    score_acts = lax.dynamic_slice_in_dim(cand_asum, own_start, own_rows, 0).astype(jnp.bfloat16)
    positions = own_start + jnp.arange(own_rows, dtype=jnp.int32)
    score_acts32 = score_acts.astype(jnp.float32)
    columns = []
    for query_index in range(Q):
        weight = (query_ids == query_index).astype(jnp.bfloat16)
        weighted = query_grads * weight[:, None]
        outer_sum = lax.dot_general(
            weighted, query_acts, (((0,), (0,)), ((), ())), preferred_element_type=jnp.float32
        )
        precond = (inverse * outer_sum).astype(jnp.bfloat16)
        projected = jnp.dot(score_grads, precond, preferred_element_type=jnp.float32)
        columns.append(jnp.sum(projected * score_acts32, axis=1))
    token_scores = jnp.stack(columns, 1)
    starts = jnp.cumsum(doc_lengths, dtype=jnp.int32) - doc_lengths
    member = (
        (positions[:, None] >= starts[None, :])
        & (positions[:, None] < (starts + doc_lengths)[None, :])
    ).astype(jnp.float32)
    partial_scores = lax.dot_general(
        member,
        token_scores,
        (((0,), (0,)), ((), ())),
        precision=lax.Precision.HIGHEST,
        preferred_element_type=jnp.float32,
    )
    return lax.psum(partial_scores, ("tok", "out", "inp"))


def solution(mesh):
    in_specs = (
        P(None, ("tok", "inp")),
        P(None, ("tok", "out")),
        P(None, ("tok", "inp")),
        P(None, ("tok", "out")),
        P(("tok", "inp"), "out"),
        P(("tok", "out"), "inp"),
        P("out", "inp"),
        P(),
        P(),
    )
    out_specs = P()
    return jax.shard_map(local, mesh=mesh, in_specs=in_specs, out_specs=out_specs, check_vma=False)
```

profile of v0, /device:TPU:1, one launch (start us, length us, event | category | flops | bytes accessed | tf_op | source)
XLA Modules:
  0.0 615.9 jit_solution(8111650596376098995)
XLA Ops:
  0.0 0.0 copy-start
  0.0 1.2 copy-done
  1.2 6.1 fusion.48
  7.2 0.0 copy-done.1
  7.2 0.0 copy-done.3
  7.3 0.0 copy-start.5
  7.3 0.0 copy-start.6
  7.3 1.2 fusion.49
  8.5 87.9 %all-reduce.4 = (bf16[256,1792]{1,0:T(8,128)(2,1)}, bf16[64,1792]{1,0:T(8,128)(2,1)}) all-reduce(f32[256,1792]{1,0:T(8,128)} %fusion.48, f32[64,1792]{1,0:T(8,128)S(1)} %fusion.49), channel_id=1, replica_groups=mesh['tok'=2,'out'=16,'inp'=8] {'tok','inp'}, use_global_device_ids=true, to_apply=%region_1.0 | all-reduce | flops 573440 | bytes 3440640 | tf_op jit(solution)/shard_map/psum | solution.py:22
  96.4 0.0 copy-done.2
  96.4 0.0 copy-done.4
  96.4 0.3 fusion.51
  96.7 0.0 copy-done.5
  96.7 0.2 fusion.50
  96.9 143.0 %all-reduce.5 = (bf16[64,1024]{1,0:T(8,128)(2,1)}, bf16[256,1024]{1,0:T(8,128)(2,1)S(1)}) all-reduce(f32[64,1024]{1,0:T(8,128)S(1)} %fusion.50, f32[256,1024]{1,0:T(8,128)S(1)} %fusion.51), channel_id=1, replica_groups=mesh['tok'=2,'out'=16,'inp'=8] {'tok','out'}, use_global_device_ids=true, to_apply=%region_5.0 | all-reduce | flops 327680 | bytes 1966080 | tf_op jit(solution)/shard_map/psum | solution.py:30
  239.9 0.0 copy-done.6
  240.0 4.5 convert_reduce_fusion
  244.5 269.3 %psum.43 = f32[]{:T(128)} all-reduce(f32[]{:T(128)} %convert_reduce_fusion), channel_id=1, replica_groups=mesh['tok'=2,'out'=16,'inp'=8] {'out','inp'}, use_global_device_ids=true, to_apply=%region_3.0 | all-reduce | flops 1 | bytes 8 | tf_op jit(solution)/shard_map/psum | solution.py:19
  514.5 0.0 copy-start.8
  514.5 0.0 copy-start.9
  514.5 0.0 copy-start.10
  514.5 4.4 fusion.9
  518.9 0.0 copy-done.8
  518.9 0.0 copy-done.9
  518.9 4.0 fusion.10
  522.9 4.0 fusion.11
  527.0 0.0 copy-start.7
  527.0 4.0 fusion.12
  531.0 0.1 copy.12
  531.2 0.1 reduce
  531.3 0.2 fusion.29
  531.5 84.4 %psum.47 = f32[16,4]{0,1:T(4,128)} all-reduce(f32[16,4]{0,1:T(4,128)S(1)} %fusion.29), channel_id=1, replica_groups=mesh['tok'=2,'out'=16,'inp'=8] {'tok','out','inp'}, use_global_device_ids=true, to_apply=%region_11.12 | all-reduce | flops 64 | bytes 512 | tf_op jit(solution)/shard_map/psum | solution.py:65
  (10 shorter events, 0.1 us)
Async XLA Ops:
  0.0 1.2 copy-start
  1.2 6.1 copy-start.1
  1.2 6.1 copy-start.3
  7.2 89.1 %copy-start.2 = (bf16[256,1024]{1,0:T(8,128)(2,1)S(1)}, bf16[256,1024]{1,0:T(8,128)(2,1)}, u32[]{:S(2)}) copy-start(bf16[256,1024]{1,0:T(8,128)(2,1)} %param.14) | copy-start | bytes 1572868
  7.2 89.1 %copy-start.4 = (bf16[256,256]{1,0:T(8,128)(2,1)S(1)}, bf16[256,256]{1,0:T(8,128)(2,1)}, u32[]{:S(2)}) copy-start(bf16[256,256]{1,0:T(8,128)(2,1)} %param.10) | copy-start | bytes 393220
  7.3 89.4 %copy-start.5 = (bf16[64,256]{1,0:T(8,128)(2,1)S(1)}, bf16[64,256]{1,0:T(8,128)(2,1)}, u32[]{:S(2)}) copy-start(bf16[64,256]{1,0:T(8,128)(2,1)} %param.12) | copy-start | bytes 98308
  7.3 232.7 %copy-start.6 = (s32[64]{0:T(128)S(1)}, s32[64]{0:T(128)}, u32[]{:S(2)}) copy-start(s32[64]{0:T(128)} %param.17) | copy-start | bytes 772
  514.5 4.4 copy-start.8
  514.5 4.4 copy-start.9
  514.5 4.4 copy-start.10
  527.0 4.1 copy-start.7
where the time goes:
time: 616 us
  blocking collectives  585 us (95%)
  matrix products  24.5 us (4%)
    psum x1, blocking collectives, local(): eigen_sum = lax.psum(jnp.sum(values), ('out', 'inp'))  269 us
    psum x1, blocking collectives, local(): lax.psum((jnp.dot(cand_act, eig_in, preferred_element_type=jnp.float32),...  143 us
    psum x1, blocking collectives, local(): lax.psum((jnp.dot(cand_grad, eig_out, preferred_element_type=jnp.float32)...  87.9 us
    psum x1, blocking collectives, local(): return lax.psum(partial_scores, ('tok', 'out', 'inp'))  84.4 us
    dot_general x4, matrix products, local(): jnp.dot(score_grads, precond, preferred_element_type=jnp.float32)  16.5 us

commit v1 on v0

v1 whole, which is shorter than its diff:
```python
import jax
import jax.numpy as jnp
from jax import lax
from jax.experimental import pallas as pl
from jax.experimental.pallas import tpu as pltpu
from jax.sharding import PartitionSpec as P

D = 8192
FF = 28672
Q = 4
MESH = pl.DeviceIdType.MESH
F32 = jnp.float32
BF16 = jnp.bfloat16
GROUPS = 7
SETS = ((0, 1024), (1024, 768))
HALF = ((0, 512), (512, 384))


def kernel(
    cg, ca, qg, qa, eo, ei, ev, dl, qi, out,
    xg, xa, eob, eib, evb, gpc, gpq, rsc, rsq, gsc, gsq, rxc, rxq, gfc, gfq,
    apc, apq, rac, raq, rdc, rdq, afc, afq, inv, mm, ea, eb, fa, fb,
    ld, evs, rs_s, rs_r, x_s, x_r, ag_s, ag_r, co_s, co_r, pr_s, pr_r, st_s, st_r,
):
    tok, o, z = lax.axis_index("tok"), lax.axis_index("out"), lax.axis_index("inp")
    x = tok * 2 + o // 8
    y = lax.rem(o // 2, 4)
    c = lax.rem(o, 2)

    def dev(dx, dy, dc, dz):
        nx = lax.rem(x + dx, 4)
        ny = lax.rem(y + dy, 4)
        nc = lax.rem(c + dc, 2)
        return (nx // 2, lax.rem(nx, 2) * 8 + ny * 2 + nc, lax.rem(z + dz, 8))

    def remote(src, dst, ss, rs, where):
        return pltpu.make_async_remote_copy(
            src_ref=src, dst_ref=dst, send_sem=ss, recv_sem=rs, device_id=where, device_id_type=MESH
        )

    def line_peer(r):
        return dev(0, 0, r // 8, lax.rem(r, 8))

    def plane_peer(r):
        return dev(r // 4, lax.rem(r, 4), 0, 0)

    def each(body):
        lax.fori_loop(1, 16, lambda r, carry: (body(r), carry)[1], 0)

    loads = [
        pltpu.make_async_copy(ca, xa.at[pl.ds(0, 256)], ld.at[0]),
        pltpu.make_async_copy(qa, xa.at[pl.ds(256, 64)], ld.at[1]),
        pltpu.make_async_copy(ei, eib, ld.at[2]),
        pltpu.make_async_copy(cg, xg.at[pl.ds(0, 256)], ld.at[3]),
        pltpu.make_async_copy(qg, xg.at[pl.ds(256, 64)], ld.at[4]),
    ]

    def eo_load(g):
        return pltpu.make_async_copy(eo.at[:, pl.ds(pl.multiple_of(g * 256, 256), 256)], eob.at[g], ld.at[5 + g])

    def ev_load(g):
        row = pl.multiple_of((2 * g + tok) * 128, 128)
        return pltpu.make_async_copy(ev.at[pl.ds(row, 128)], evb.at[g], evs.at[g])

    for load in loads:
        load.start()
    for g in range(GROUPS):
        eo_load(g).start()

    barrier = pltpu.get_barrier_semaphore()

    def greet(r):
        pl.semaphore_signal(barrier, inc=1, device_id=line_peer(r), device_id_type=MESH)
        pl.semaphore_signal(barrier, inc=1, device_id=plane_peer(r), device_id_type=MESH)

    each(greet)
    for g in range(GROUPS):
        ev_load(g).start()

    for load in loads[:3]:
        load.wait()
    apart = jnp.dot(xa[...], eib[...], preferred_element_type=F32)
    apc[...] = apart[:256].astype(BF16)
    apq[...] = apart[256:]

    pl.semaphore_wait(barrier, 30)

    other = pl.ds(pl.multiple_of((1 - c) * 512, 512), 512)
    mine = pl.ds(pl.multiple_of(c * 512, 512), 512)
    core1 = [
        remote(apc.at[:, other], rac, co_s.at[0], co_r.at[0], dev(0, 0, 1, 0)),
        remote(apq.at[:, other], raq, co_s.at[1], co_r.at[1], dev(0, 0, 1, 0)),
    ]
    for copy in core1:
        copy.start()

    for load in loads[3:]:
        load.wait()

    def rotate(g, carry):
        eo_load(g).wait()
        part = jnp.dot(xg[...], eob[g], preferred_element_type=F32)
        cols = pl.ds(pl.multiple_of(g * 256, 256), 256)
        gpc[:, cols] = part[:256].astype(BF16)
        gpq[:, cols] = part[256:]
        return carry

    part_refs = (gpq, gpc)
    ring_refs = (rsq, rsc)
    heights = (8, 32)

    def rows(kind, owner):
        h = heights[kind]
        return pl.ds(pl.multiple_of(lax.rem(owner + 16, 8) * h, h), h)

    def hop(d):
        return dev(0, 0, 0, 1 if d == 0 else 7)

    def sign(d):
        return 1 if d == 0 else -1

    def rs_first(kind, d, s, cs):
        cols = pl.ds(*SETS[cs])
        return remote(
            part_refs[kind].at[rows(kind, z + sign(d) * (5 - s)), cols],
            ring_refs[kind].at[d, s - 1, :, cols],
            rs_s.at[kind, d, s - 1, cs], rs_r.at[kind, d, s - 1, cs], hop(d),
        )

    def rs_next(kind, d, s, cs):
        cols = pl.ds(*SETS[cs])
        return remote(
            ring_refs[kind].at[d, s - 2, :, cols],
            ring_refs[kind].at[d, s - 1, :, cols],
            rs_s.at[kind, d, s - 1, cs], rs_r.at[kind, d, s - 1, cs], hop(d),
        )

    def rs_copy(kind, d, s, cs):
        first = 1 if cs == d else 2
        return rs_first(kind, d, s, cs) if s == first else rs_next(kind, d, s, cs)

    def rs_step(kind, s):
        for d in range(2):
            for cs in ((d, 1 - d) if s > 1 else (d,)):
                rs_copy(kind, d, s, cs).wait_recv()
                cols = pl.ds(*SETS[cs])
                ref = ring_refs[kind]
                own = part_refs[kind][rows(kind, z + sign(d) * (4 - s)), cols].astype(F32)
                ref[d, s - 1, :, cols] = (ref[d, s - 1, :, cols].astype(F32) + own).astype(ref.dtype)
                rs_copy(kind, d, s + 1, cs).start()

    lax.fori_loop(0, 4, rotate, 0)
    for kind in range(2):
        rs_copy(kind, 0, 1, 0).start()
        rs_copy(kind, 1, 2, 0).start()
    lax.fori_loop(4, 7, rotate, 0)
    for kind in range(2):
        rs_copy(kind, 1, 1, 1).start()
        rs_copy(kind, 0, 2, 1).start()

    for copy in core1:
        copy.wait()
    rac[...] = (rac[...].astype(F32) + apc[:, mine].astype(F32)).astype(BF16)
    raq[...] = raq[...] + apq[:, mine]
    chip = x * 4 + y

    def a_scatter(r):
        nx = lax.rem(x + r // 4, 4)
        ny = lax.rem(y + lax.rem(r, 4), 4)
        cols = pl.ds(pl.multiple_of(ny * 128, 128), 128)
        return (
            remote(rac.at[pl.ds(pl.multiple_of(nx * 64, 64), 64), cols], rdc.at[chip],
                   pr_s.at[0, r], pr_r.at[0, r], plane_peer(r)),
            remote(raq.at[pl.ds(pl.multiple_of(nx * 16, 16), 16), cols], rdq.at[chip],
                   pr_s.at[1, r], pr_r.at[1, r], plane_peer(r)),
        )

    def start_both(pair):
        pair[0].start()
        pair[1].start()

    def recv_both(pair):
        pair[0].wait_recv()
        pair[1].wait_recv()

    def send_both(pair):
        pair[0].wait_send()
        pair[1].wait_send()

    each(lambda r: start_both(a_scatter(r)))
    own_rows_c = pl.ds(pl.multiple_of(x * 64, 64), 64)
    own_rows_q = pl.ds(pl.multiple_of(x * 16, 16), 16)
    own_cols = pl.ds(pl.multiple_of(y * 128, 128), 128)
    rdc[chip] = rac[own_rows_c, own_cols]
    rdq[chip] = raq[own_rows_q, own_cols]

    for kind in range(2):
        rs_step(kind, 1)

    line = c * 8 + z
    total = jnp.zeros((8, 128), F32)
    for g in range(GROUPS):
        ev_load(g).wait()
        for cb in range(8):
            vals = evb[g, :, cb * 128:(cb + 1) * 128].astype(F32)
            total = total + jnp.sum(vals.reshape(16, 8, 128), axis=0)

    def all_to(buf, slot, kind, peer):
        def body(r):
            return remote(buf.at[slot], buf.at[slot], st_s.at[kind, r], st_r.at[kind, r], peer(r))
        return body

    e_line = all_to(ea, line, 0, line_peer)
    e_plane = all_to(eb, chip, 1, plane_peer)
    f_line = all_to(fa, line, 2, line_peer)
    f_plane = all_to(fb, chip, 3, plane_peer)

    ea[line] = total
    each(lambda r: e_line(r).start())

    for kind in range(2):
        rs_step(kind, 2)

    each(lambda r: e_line(r).wait_recv())
    eb[chip] = jnp.sum(ea[...], axis=0)
    each(lambda r: e_plane(r).start())

    each(lambda r: recv_both(a_scatter(r)))
    piece_cols = pl.ds(pl.multiple_of(c * 512 + y * 128, 128), 128)
    afc[own_rows_c, piece_cols] = jnp.sum(rdc[...].astype(F32), axis=0).astype(BF16)
    afq[own_rows_q, piece_cols] = jnp.sum(rdq[...], axis=0).astype(BF16)

    def a_gather(r):
        return (
            remote(afc.at[own_rows_c, piece_cols], afc.at[own_rows_c, piece_cols],
                   pr_s.at[2, r], pr_r.at[2, r], plane_peer(r)),
            remote(afq.at[own_rows_q, piece_cols], afq.at[own_rows_q, piece_cols],
                   pr_s.at[3, r], pr_r.at[3, r], plane_peer(r)),
        )

    each(lambda r: start_both(a_gather(r)))

    for kind in range(2):
        rs_step(kind, 3)

    each(lambda r: e_plane(r).wait_recv())
    eigen_sum = jnp.sum(jnp.sum(eb[...], axis=0))
    damping = 0.1 * eigen_sum / (FF * D)

    def invert(g, carry):
        inv[g] = 1.0 / (evb[g].astype(F32) + damping)
        return carry

    lax.fori_loop(0, GROUPS, invert, 0)

    sum_refs = (gsq, gsc)
    x_refs = (rxq, rxc)
    full_refs = (gfq, gfc)

    def x_copy(kind, cs):
        cols = pl.ds(*HALF[cs])
        return remote(sum_refs[kind].at[1 - tok, :, cols], x_refs[kind].at[:, cols],
                      x_s.at[kind, cs], x_r.at[kind, cs], dev(2, 0, 0, 0))

    for kind in range(2):
        for cs in range(2):
            rs_copy(kind, 0, 4, cs).wait_recv()
            rs_copy(kind, 1, 4, cs).wait_recv()
            lo, size = SETS[cs]
            for g in range(lo // 256, (lo + size) // 256):
                for t in range(2):
                    cols = pl.ds(g * 256 + t * 128, 128)
                    value = (
                        part_refs[kind][rows(kind, z), cols].astype(F32)
                        + ring_refs[kind][0, 3, :, cols].astype(F32)
                        + ring_refs[kind][1, 3, :, cols].astype(F32)
                    )
                    sum_refs[kind][t, :, g * 128:(g + 1) * 128] = value.astype(sum_refs[kind].dtype)
            x_copy(kind, cs).start()

    def ag_copy(kind, d, s, cs):
        cols = pl.ds(*HALF[cs])
        at = rows(kind, z - sign(d) * (s - 1))
        return remote(full_refs[kind].at[at, cols], full_refs[kind].at[at, cols],
                      ag_s.at[kind, d, s - 1, cs], ag_r.at[kind, d, s - 1, cs], hop(d))

    for kind in range(2):
        for cs in range(2):
            x_copy(kind, cs).wait_recv()
            cols = pl.ds(*HALF[cs])
            value = sum_refs[kind][tok, :, cols].astype(F32) + x_refs[kind][:, cols].astype(F32)
            full_refs[kind][rows(kind, z), cols] = value.astype(BF16).astype(full_refs[kind].dtype)
            for d in range(2):
                ag_copy(kind, d, 1, cs).start()

    each(lambda r: recv_both(a_gather(r)))
    core2 = [
        remote(afc.at[:, mine], afc.at[:, mine], co_s.at[2], co_r.at[2], dev(0, 0, 1, 0)),
        remote(afq.at[:, mine], afq.at[:, mine], co_s.at[3], co_r.at[3], dev(0, 0, 1, 0)),
    ]
    for copy in core2:
        copy.start()

    ids = jnp.zeros((1, 64), jnp.int32)
    lane = lax.broadcasted_iota(jnp.int32, (1, 64), 1)
    for s in range(64):
        ids = jnp.where(lane == s, qi[s], ids)
    doc = lax.broadcasted_iota(jnp.int32, (16, 256), 0)
    position = lax.broadcasted_iota(jnp.int32, (16, 256), 1)
    first = jnp.zeros((16, 256), jnp.int32)
    last = jnp.zeros((16, 256), jnp.int32)
    start = jnp.int32(0)
    for n in range(16):
        stop = start + dl[n]
        first = jnp.where(doc == n, start, first)
        last = jnp.where(doc == n, stop, last)
        start = stop
    member = ((position >= first) & (position < last)).astype(F32)

    def ag_step(kind, s):
        for d in range(2):
            for cs in ((d, 1 - d) if s < 4 else (d,)):
                ag_copy(kind, d, s, cs).wait_recv()
                if s < 3 or (s == 3 and cs == d):
                    ag_copy(kind, d, s + 1, cs).start()

    for s in (1, 2, 3):
        for kind in range(2):
            ag_step(kind, s)
    for copy in core2:
        copy.wait()
    ag_step(0, 4)

    def contract(g, carry):
        cols = pl.ds(pl.multiple_of(g * 128, 128), 128)
        turned = gfq[:, cols].T
        stacked = jnp.concatenate(
            [jnp.where(ids == q, turned, 0.0).astype(BF16) for q in range(Q)], axis=0
        )
        outer = jnp.dot(stacked, afq[...], preferred_element_type=F32)
        scale = inv[g]
        precond = jnp.concatenate(
            [(scale * outer[q * 128:(q + 1) * 128]).astype(BF16) for q in range(Q)], axis=0
        )
        mm[g] = lax.dot_general(
            afc[...], precond, (((1,), (1,)), ((), ())), preferred_element_type=F32
        )
        return carry

    lax.fori_loop(0, GROUPS, contract, 0)
    ag_step(1, 4)

    columns = []
    for q in range(Q):
        acc = jnp.zeros((256, 128), F32)
        for g in range(GROUPS):
            acc = acc + gfc[:, g * 128:(g + 1) * 128].astype(F32) * mm[g, :, q * 128:(q + 1) * 128]
        columns.append(acc)
    spread = jnp.dot(
        member, jnp.concatenate(columns, axis=1), precision=lax.Precision.HIGHEST, preferred_element_type=F32
    )
    lanes = lax.broadcasted_iota(jnp.int32, (16, 128), 1)
    scores = jnp.zeros((16, 128), F32)
    for q in range(Q):
        column = jnp.sum(spread[:, q * 128:(q + 1) * 128], axis=1, keepdims=True)
        scores = jnp.where(lanes == q, column, scores)

    fa[line] = scores
    each(lambda r: f_line(r).start())
    each(lambda r: f_line(r).wait_recv())
    fb[chip] = jnp.sum(fa[...], axis=0)
    each(lambda r: f_plane(r).start())
    each(lambda r: f_plane(r).wait_recv())
    out[...] = jnp.sum(fb[...], axis=0)[:, :Q]

    for kind in range(2):
        for cs in range(2):
            x_copy(kind, cs).wait_send()
        for d in range(2):
            for s in range(1, 5):
                for cs in range(2):
                    if s > 1 or cs == d:
                        rs_copy(kind, d, s, cs).wait_send()
                    if s < 4 or cs == d:
                        ag_copy(kind, d, s, cs).wait_send()

    def drain(r):
        send_both(a_scatter(r))
        send_both(a_gather(r))
        for body in (e_line, e_plane, f_line, f_plane):
            body(r).wait_send()

    each(drain)


def local(*args):
    dma = pltpu.SemaphoreType.DMA
    vm = pltpu.VMEM
    return pl.pallas_call(
        kernel,
        out_shape=jax.ShapeDtypeStruct((16, Q), F32),
        in_specs=[pl.BlockSpec(memory_space=pl.ANY)] * 7 + [pl.BlockSpec(memory_space=pltpu.SMEM)] * 2,
        out_specs=pl.BlockSpec(memory_space=pltpu.VMEM),
        scratch_shapes=[
            vm((320, 1792), BF16), vm((320, 256), BF16), vm((GROUPS, 1792, 256), BF16), vm((256, 1024), BF16),
            vm((GROUPS, 128, 1024), BF16),
            vm((256, 1792), BF16), vm((64, 1792), F32),
            vm((2, 4, 32, 1792), BF16), vm((2, 4, 8, 1792), F32),
            vm((2, 32, 896), BF16), vm((2, 8, 896), F32),
            vm((32, 896), BF16), vm((8, 896), F32),
            vm((256, 896), BF16), vm((64, 896), F32),
            vm((256, 1024), BF16), vm((64, 1024), F32),
            vm((256, 512), BF16), vm((64, 512), F32),
            vm((16, 64, 128), BF16), vm((16, 16, 128), F32),
            vm((256, 1024), BF16), vm((64, 1024), BF16),
            vm((GROUPS, 128, 1024), F32), vm((GROUPS, 256, 512), F32),
            vm((16, 8, 128), F32), vm((16, 8, 128), F32), vm((16, 16, 128), F32), vm((16, 16, 128), F32),
            dma((5 + GROUPS,)), dma((GROUPS,)),
            dma((2, 2, 4, 2)), dma((2, 2, 4, 2)),
            dma((2, 2)), dma((2, 2)),
            dma((2, 2, 4, 2)), dma((2, 2, 4, 2)),
            dma((4,)), dma((4,)),
            dma((4, 16)), dma((4, 16)),
            dma((4, 16)), dma((4, 16)),
        ],
        name="influence",
        compiler_params=pltpu.CompilerParams(
            collective_id=0, has_side_effects=True, vmem_limit_bytes=52 << 20
        ),
    )(*args)


def solution(mesh):
    in_specs = (
        P(None, ("tok", "inp")),
        P(None, ("tok", "out")),
        P(None, ("tok", "inp")),
        P(None, ("tok", "out")),
        P(("tok", "inp"), "out"),
        P(("tok", "out"), "inp"),
        P("out", "inp"),
        P(),
        P(),
    )
    return jax.shard_map(local, mesh=mesh, in_specs=in_specs, out_specs=P(), check_vma=False)
```

time: 616 us -> 75.3 us (0.12)
  blocking collectives: 585 us -> 0 us
  Pallas kernels: 0 us -> 68.2 us
  matrix products: 24.5 us -> 0 us
    psum x4 -> x0, blocking collectives: 585 us -> none  [the longest x1 269 us: local(): eigen_sum = lax.psum(jnp.sum(values), ('out', 'inp'))]
    pallas_call x0 -> x1, Pallas kernels: none -> 68.2 us  [local(): pl.pallas_call(kernel, out_shape=jax.ShapeDtypeStruct((16, Q), F32), in_s...]
    dot_general x9 -> x0, matrix products: 24.5 us -> none  [the longest x4 16.5 us: local(): jnp.dot(score_grads, precond, preferred_element_type=jnp.float32)]
where the time goes in v1:
time: 75.3 us; the launch traced here: 75 us
  Pallas kernels  68.2 us (91%)
  local copies, waits for them, and re-layouts  6.78 us (9%)
    pallas_call x1, Pallas kernels, local(): pl.pallas_call(kernel, out_shape=jax.ShapeDtypeStruct((16, Q), F32), in_s...  68.2 us
    unnamed x14, local copies, waits for them, and re-layouts  6.13 us

profile of v1, /device:TPU:1, one launch (start us, length us, event | category | flops | bytes accessed | tf_op | source)
XLA Modules:
  0.0 75.0 jit_solution(14257549222925862854)
XLA Ops:
  0.0 0.0 copy-start
  0.0 1.2 %copy-done = bf16[256,1792]{1,0:T(8,128)(2,1)S(1)} copy-done((bf16[256,1792]{1,0:T(8,128)(2,1)S(1)}, bf16[256,1792]{1,0:T(8,128)(2,1)}, u32[]{:S(2)}) %copy-start) | copy-done | bytes 917528
  1.2 0.0 copy-start.1
  1.2 1.0 %copy-done.1 = bf16[256,1024]{1,0:T(8,128)(2,1)S(1)} copy-done((bf16[256,1024]{1,0:T(8,128)(2,1)S(1)}, bf16[256,1024]{1,0:T(8,128)(2,1)}, u32[]{:S(2)}) %copy-start.1) | copy-done | bytes 524312
  2.2 0.0 copy-start.2
  2.2 0.9 %copy-done.2 = bf16[64,1792]{1,0:T(8,128)(2,1)S(1)} copy-done((bf16[64,1792]{1,0:T(8,128)(2,1)S(1)}, bf16[64,1792]{1,0:T(8,128)(2,1)}, u32[]{:S(2)}) %copy-start.2) | copy-done | bytes 229400
  3.2 0.0 copy-start.3
  3.2 0.9 %copy-done.3 = bf16[256,256]{1,0:T(8,128)(2,1)S(1)} copy-done((bf16[256,256]{1,0:T(8,128)(2,1)S(1)}, bf16[256,256]{1,0:T(8,128)(2,1)}, u32[]{:S(2)}) %copy-start.3) | copy-done | bytes 131096
  4.1 0.0 copy-start.4
  4.1 0.8 %copy-done.4 = bf16[64,256]{1,0:T(8,128)(2,1)S(1)} copy-done((bf16[64,256]{1,0:T(8,128)(2,1)S(1)}, bf16[64,256]{1,0:T(8,128)(2,1)}, u32[]{:S(2)}) %copy-start.4) | copy-done | bytes 32792
  4.8 0.0 copy-start.5
  4.8 0.7 copy-done.5
  5.5 0.0 copy-start.6
  5.5 0.7 copy-done.6
  6.1 68.2 %influence.1 = f32[16,4]{1,0:T(8,128)S(1)} custom-call(bf16[256,1792]{1,0:T(8,128)(2,1)S(1)} %copy-done, bf16[256,256]{1,0:T(8,128)(2,1)S(1)} %copy-done.3, bf16[64,1792]{1,0:T(8,128)(2,1)S(1)} %copy-done.2, bf16[64,256]{1,0:T(8,128)(2,1)S(1)} %copy-done.4, bf16[1792,1792]{1,0:T(8,128)(2,1)} %eo.1, bf16[256,1024]{1,0:T(8,128)(2,1)S(1)} %copy-done.1, ...), custom_call_target="tpu_custom_call" | custom-call | tf_op jit(solution)/shard_map/influence/pallas_call | solution.py:399
  74.3 0.7 copy.10
Async XLA Ops:
  0.0 1.2 %copy-start = (bf16[256,1792]{1,0:T(8,128)(2,1)S(1)}, bf16[256,1792]{1,0:T(8,128)(2,1)}, u32[]{:S(2)}) copy-start(bf16[256,1792]{1,0:T(8,128)(2,1)} %cg.1) | copy-start | bytes 2752516
  1.2 1.0 %copy-start.1 = (bf16[256,1024]{1,0:T(8,128)(2,1)S(1)}, bf16[256,1024]{1,0:T(8,128)(2,1)}, u32[]{:S(2)}) copy-start(bf16[256,1024]{1,0:T(8,128)(2,1)} %ei.1) | copy-start | bytes 1572868
  2.2 0.9 %copy-start.2 = (bf16[64,1792]{1,0:T(8,128)(2,1)S(1)}, bf16[64,1792]{1,0:T(8,128)(2,1)}, u32[]{:S(2)}) copy-start(bf16[64,1792]{1,0:T(8,128)(2,1)} %qg.1) | copy-start | bytes 688132
  3.2 0.9 %copy-start.3 = (bf16[256,256]{1,0:T(8,128)(2,1)S(1)}, bf16[256,256]{1,0:T(8,128)(2,1)}, u32[]{:S(2)}) copy-start(bf16[256,256]{1,0:T(8,128)(2,1)} %ca.1) | copy-start | bytes 393220
  4.1 0.8 %copy-start.4 = (bf16[64,256]{1,0:T(8,128)(2,1)S(1)}, bf16[64,256]{1,0:T(8,128)(2,1)}, u32[]{:S(2)}) copy-start(bf16[64,256]{1,0:T(8,128)(2,1)} %qa.1) | copy-start | bytes 98308
  4.8 0.7 copy-start.5
  5.5 0.7 copy-start.6

commit v2 on v1

v2 whole, which is shorter than its diff:
```python
import jax
import jax.numpy as jnp
from jax import lax
from jax.experimental import pallas as pl
from jax.experimental.pallas import tpu as pltpu
from jax.sharding import PartitionSpec as P

D = 8192
FF = 28672
Q = 4
MESH = pl.DeviceIdType.MESH
F32 = jnp.float32
BF16 = jnp.bfloat16
GROUPS = 7
SETS = ((0, 512), (512, 384))


def kernel(
    cg, ca, qg, qa, eo, ei, ev, dl, qi, out,
    xg, xa, eob, eib, evb, gpc, gpq, rsc, rsq, oxc, oxq, gfc, gfq,
    apc, apq, rac, raq, rdc, rdq, afc, afq, inv, mm, ea, eb, fa, fb,
    ld, evs, rs_s, rs_r, ag_s, ag_r, co_s, co_r, pr_s, pr_r, st_s, st_r,
):
    tok, o, z = lax.axis_index("tok"), lax.axis_index("out"), lax.axis_index("inp")
    x = tok * 2 + o // 8
    y = lax.rem(o // 2, 4)
    c = lax.rem(o, 2)
    chip = x * 4 + y
    line = c * 8 + z

    def dev(dx, dy, dc, dz):
        nx = lax.rem(x + dx, 4)
        ny = lax.rem(y + dy, 4)
        nc = lax.rem(c + dc, 2)
        return (nx // 2, lax.rem(nx, 2) * 8 + ny * 2 + nc, lax.rem(z + dz, 8))

    def remote(src, dst, ss, rs, where):
        return pltpu.make_async_remote_copy(
            src_ref=src, dst_ref=dst, send_sem=ss, recv_sem=rs, device_id=where, device_id_type=MESH
        )

    def line_peer(r):
        n = r - 1 + r // 15
        j = n // 2
        odd = lax.rem(j, 2)
        dz = 4 + odd * ((j + 1) // 2) + (1 - odd) * (8 - j // 2)
        return dev(0, 0, lax.rem(n, 2), dz)

    def plane_shift(r):
        n = r - 1 + r // 11
        return lax.rem(2 + n // 4, 4), lax.rem(2 + lax.rem(n, 4), 4)

    def plane_peer(r):
        dx, dy = plane_shift(r)
        return dev(dx, dy, 0, 0)

    def each(body):
        lax.fori_loop(1, 16, lambda r, carry: (body(r), carry)[1], 0)

    sends, waits = [], {}

    def single(copy):
        return lambda do: do(copy)

    def several(copies):
        def run(do):
            for copy in copies:
                do(copy)
        return run

    def bundle(copies):
        def run(do):
            def body(r):
                for copy in copies(r):
                    do(copy)
            each(body)
        return run

    def send(key, run):
        run(lambda copy: copy.start())
        sends.append(run)
        waits[key] = run

    def arrive(key):
        waits.pop(key)(lambda copy: copy.wait_recv())

    def drain():
        while sends:
            sends.pop()(lambda copy: copy.wait_send())

    def finish():
        for key in list(waits):
            arrive(key)
        drain()

    loads = [
        pltpu.make_async_copy(ca, xa.at[pl.ds(0, 256)], ld.at[0]),
        pltpu.make_async_copy(qa, xa.at[pl.ds(256, 64)], ld.at[1]),
        pltpu.make_async_copy(ei, eib, ld.at[2]),
        pltpu.make_async_copy(cg, xg.at[pl.ds(0, 256)], ld.at[3]),
        pltpu.make_async_copy(qg, xg.at[pl.ds(256, 64)], ld.at[4]),
    ]

    def eo_load(g):
        return pltpu.make_async_copy(eo.at[:, pl.ds(pl.multiple_of(g * 256, 256), 256)], eob.at[g], ld.at[5 + g])

    def ev_load(g):
        row = pl.multiple_of((2 * g + tok) * 128, 128)
        return pltpu.make_async_copy(ev.at[pl.ds(row, 128)], evb.at[g], evs.at[g])

    for load in loads:
        load.start()
    for g in range(GROUPS):
        eo_load(g).start()

    barrier = pltpu.get_barrier_semaphore()

    def greet(r):
        pl.semaphore_signal(barrier, inc=1, device_id=line_peer(r), device_id_type=MESH)
        pl.semaphore_signal(barrier, inc=1, device_id=plane_peer(r), device_id_type=MESH)

    each(greet)
    for g in range(GROUPS):
        ev_load(g).start()

    for load in loads[:3]:
        load.wait()
    apart = jnp.dot(xa[...], eib[...], preferred_element_type=F32)
    apc[...] = apart[:256].astype(BF16)
    apq[...] = apart[256:]

    for load in loads[3:]:
        load.wait()
    gpq[:, 1, :, 384:] = jnp.zeros((2, 64, 128), BF16)

    def rotate(g):
        eo_load(g).wait()
        part = jnp.dot(xg[...], eob[g], preferred_element_type=F32).astype(BF16)
        for t in range(2):
            gpc[t, :, g * 128:(g + 1) * 128] = part[:256, t * 128:(t + 1) * 128]
            gpq[t, g // 4, :, (g % 4) * 128:(g % 4 + 1) * 128] = part[256:, t * 128:(t + 1) * 128]

    def c_rows(owner):
        return pl.ds(pl.multiple_of(lax.rem(owner + 16, 8) * 32, 32), 32)

    def q_rows(owner):
        return pl.ds(pl.multiple_of(lax.rem(owner + 16, 8) // 2 * 16, 16), 16)

    def q_cols(owner):
        return pl.ds(pl.multiple_of(lax.rem(owner + 16, 2) * 256, 256), 256)

    def own_part(kind, t, owner, cs):
        if kind == 0:
            return gpq.at[t, cs, q_rows(owner), q_cols(owner)]
        return gpc.at[t, c_rows(owner), pl.ds(*SETS[cs])]

    def slot(kind, d, s, t, cs):
        if kind == 0:
            return rsq.at[d, s - 1, t, cs]
        return rsc.at[d, s - 1, t, :, pl.ds(*SETS[cs])]

    def sign(d):
        return 1 if d == 0 else -1

    BOTH = slice(None)

    def rs_copies(kind, d, s, cs):
        first = 1 if cs == d else 2
        dz = 1 if d == 0 else 7
        if s < 4:
            if s == first:
                src = own_part(kind, BOTH, z + sign(d) * (5 - s), cs)
            else:
                src = slot(kind, d, s - 1, BOTH, cs)
            return [remote(src, slot(kind, d, s, BOTH, cs), rs_s.at[kind, d, s - 1, cs],
                           rs_r.at[kind, d, s - 1, cs], dev(0, 0, 0, dz))]
        return [
            remote(slot(kind, d, 3, t, cs), slot(kind, d, 4, j, cs), rs_s.at[kind, d, 3 + j, cs],
                   rs_r.at[kind, d, 3 + j, cs], dev(2 * j, 0, 0, dz))
            for j, t in ((1, 1 - tok), (0, tok))
        ]

    def rs_send(kind, d, s, cs):
        send(("rs", kind, d, s, cs), several(rs_copies(kind, d, s, cs)))

    def rs_step(kind, s):
        for n in range(2 if s > 1 else 1):
            for d in range(2):
                cs = d if n == 0 else 1 - d
                arrive(("rs", kind, d, s, cs))
                held = slot(kind, d, s, BOTH, cs)
                own = own_part(kind, BOTH, z + sign(d) * (4 - s), cs)
                held[...] = (held[...].astype(F32) + own[...].astype(F32)).astype(BF16)
                rs_send(kind, d, s + 1, cs)

    for g in range(4):
        rotate(g)
    pl.semaphore_wait(barrier, 30)
    for kind in range(2):
        rs_send(kind, 0, 1, 0)
        rs_send(kind, 1, 2, 0)
    other = pl.ds(pl.multiple_of((1 - c) * 512, 512), 512)
    mine = pl.ds(pl.multiple_of(c * 512, 512), 512)
    send("core 1", several([
        remote(apc.at[:, other], rac, co_s.at[0], co_r.at[0], dev(0, 0, 1, 0)),
        remote(apq.at[:, other], raq, co_s.at[1], co_r.at[1], dev(0, 0, 1, 0)),
    ]))
    for g in range(4, 7):
        rotate(g)
    for kind in range(2):
        rs_send(kind, 1, 1, 1)
        rs_send(kind, 0, 2, 1)
    send("own", several([
        remote(gpq.at[1 - tok, :, q_rows(z), q_cols(z)], oxq, co_s.at[4], co_r.at[4], dev(2, 0, 0, 0)),
        remote(gpc.at[1 - tok, c_rows(z)], oxc, co_s.at[5], co_r.at[5], dev(2, 0, 0, 0)),
    ]))

    arrive("core 1")
    rac[...] = (rac[...].astype(F32) + apc[:, mine].astype(F32)).astype(BF16)
    raq[...] = raq[...] + apq[:, mine]

    def a_scatter(r):
        dx, dy = plane_shift(r)
        nx = lax.rem(x + dx, 4)
        cols = pl.ds(pl.multiple_of(lax.rem(y + dy, 4) * 128, 128), 128)
        return (
            remote(rac.at[pl.ds(pl.multiple_of(nx * 64, 64), 64), cols], rdc.at[chip],
                   pr_s.at[0, r], pr_r.at[0, r], plane_peer(r)),
            remote(raq.at[pl.ds(pl.multiple_of(nx * 16, 16), 16), cols], rdq.at[chip],
                   pr_s.at[1, r], pr_r.at[1, r], plane_peer(r)),
        )

    send("scatter", bundle(a_scatter))
    own_rows_c = pl.ds(pl.multiple_of(x * 64, 64), 64)
    own_rows_q = pl.ds(pl.multiple_of(x * 16, 16), 16)
    own_cols = pl.ds(pl.multiple_of(y * 128, 128), 128)
    rdc[chip] = rac[own_rows_c, own_cols]
    rdq[chip] = raq[own_rows_q, own_cols]

    for kind in range(2):
        rs_step(kind, 1)

    total = jnp.zeros((8, 128), F32)
    for g in range(GROUPS):
        ev_load(g).wait()
        for cb in range(8):
            vals = evb[g, :, cb * 128:(cb + 1) * 128].astype(F32)
            total = total + jnp.sum(vals.reshape(16, 8, 128), axis=0)

    def all_to(buf, place, kind, peer):
        def body(r):
            return [remote(buf.at[place], buf.at[place], st_s.at[kind, r], st_r.at[kind, r], peer(r))]
        return bundle(body)

    ea[line] = jnp.sum(total, axis=0, keepdims=True)
    send("e line", all_to(ea, line, 0, line_peer))

    for kind in range(2):
        rs_step(kind, 2)

    arrive("e line")
    eb[chip] = jnp.sum(ea[...], axis=0)
    send("e plane", all_to(eb, chip, 1, plane_peer))

    arrive("scatter")
    piece_cols = pl.ds(pl.multiple_of(c * 512 + y * 128, 128), 128)
    afc[own_rows_c, piece_cols] = jnp.sum(rdc[...].astype(F32), axis=0).astype(BF16)
    afq[own_rows_q, piece_cols] = jnp.sum(rdq[...], axis=0).astype(BF16)

    def a_gather(r):
        return (
            remote(afc.at[own_rows_c, piece_cols], afc.at[own_rows_c, piece_cols],
                   pr_s.at[2, r], pr_r.at[2, r], plane_peer(r)),
            remote(afq.at[own_rows_q, piece_cols], afq.at[own_rows_q, piece_cols],
                   pr_s.at[3, r], pr_r.at[3, r], plane_peer(r)),
        )

    send("gather", bundle(a_gather))

    for kind in range(2):
        rs_step(kind, 3)

    arrive("own")

    def full_part(kind, owner, cs):
        if kind == 0:
            return gfq.at[cs, q_rows(owner), q_cols(owner)]
        return gfc.at[c_rows(owner), pl.ds(*SETS[cs])]

    def ag_copy(kind, d, s, cs):
        part = full_part(kind, z - sign(d) * (s - 1), cs)
        return remote(part, part, ag_s.at[kind, d, s - 1, cs], ag_r.at[kind, d, s - 1, cs],
                      dev(0, 0, 0, 1 if d == 0 else 7))

    def ag_send(kind, d, s, cs):
        send(("ag", kind, d, s, cs), single(ag_copy(kind, d, s, cs)))

    def owner_sum(kind):
        for cs in range(2):
            arrive(("rs", kind, 0, 4, cs))
            arrive(("rs", kind, 1, 4, cs))
            value = own_part(kind, tok, z, cs)[...].astype(F32)
            value = value + (oxq[cs] if kind == 0 else oxc[:, pl.ds(*SETS[cs])]).astype(F32)
            for d in range(2):
                for j in range(2):
                    value = value + slot(kind, d, 4, j, cs)[...].astype(F32)
            full_part(kind, z, cs)[...] = value.astype(BF16)
            for d in range(2):
                ag_send(kind, d, 1, cs)

    owner_sum(0)
    owner_sum(1)

    arrive("e plane")
    eigen_sum = jnp.sum(jnp.sum(eb[...], axis=0))
    damping = 0.1 * eigen_sum / (FF * D)

    def invert(g, carry):
        inv[g] = 1.0 / (evb[g].astype(F32) + damping)
        return carry

    lax.fori_loop(0, GROUPS, invert, 0)

    def ag_step(kind, s):
        for n in range(2 if s < 4 else 1):
            for d in range(2):
                cs = d if n == 0 else 1 - d
                arrive(("ag", kind, d, s, cs))
                if s < 3 or (s == 3 and cs == d):
                    ag_send(kind, d, s + 1, cs)

    ag_step(0, 1)
    arrive("gather")
    send("core 2", several([
        remote(afc.at[:, mine], afc.at[:, mine], co_s.at[2], co_r.at[2], dev(0, 0, 1, 0)),
        remote(afq.at[:, mine], afq.at[:, mine], co_s.at[3], co_r.at[3], dev(0, 0, 1, 0)),
    ]))
    ag_step(1, 1)

    ids = jnp.zeros((1, 64), jnp.int32)
    lane = lax.broadcasted_iota(jnp.int32, (1, 64), 1)
    for s in range(64):
        ids = jnp.where(lane == s, qi[s], ids)
    doc = lax.broadcasted_iota(jnp.int32, (16, 256), 0)
    position = lax.broadcasted_iota(jnp.int32, (16, 256), 1)
    first = jnp.zeros((16, 256), jnp.int32)
    last = jnp.zeros((16, 256), jnp.int32)
    start = jnp.int32(0)
    for n in range(16):
        stop = start + dl[n]
        first = jnp.where(doc == n, start, first)
        last = jnp.where(doc == n, stop, last)
        start = stop
    member = ((position >= first) & (position < last)).astype(F32)

    ag_step(0, 2)
    ag_step(1, 2)
    ag_step(0, 3)
    arrive("core 2")
    ag_step(0, 4)

    def contract(g, carry):
        cols = pl.ds(pl.multiple_of(lax.rem(g, 4) * 128, 128), 128)
        turned = gfq[g // 4, :, cols].astype(F32).T
        stacked = jnp.concatenate(
            [jnp.where(ids == q, turned, 0.0).astype(BF16) for q in range(Q)], axis=0
        )
        outer = jnp.dot(stacked, afq[...], preferred_element_type=F32)
        scale = inv[g]
        precond = jnp.concatenate(
            [(scale * outer[q * 128:(q + 1) * 128]).astype(BF16) for q in range(Q)], axis=0
        )
        mm[g] = lax.dot_general(
            afc[...], precond, (((1,), (1,)), ((), ())), preferred_element_type=F32
        )
        return carry

    lax.fori_loop(0, 2, contract, 0)
    ag_step(1, 3)
    lax.fori_loop(2, GROUPS, contract, 0)
    ag_step(1, 4)

    columns = []
    for q in range(Q):
        acc = jnp.zeros((256, 128), F32)
        for g in range(GROUPS):
            acc = acc + gfc[:, g * 128:(g + 1) * 128].astype(F32) * mm[g, :, q * 128:(q + 1) * 128]
        columns.append(acc)
    spread = jnp.dot(
        member, jnp.concatenate(columns, axis=1), precision=lax.Precision.HIGHEST, preferred_element_type=F32
    )
    column = lax.broadcasted_iota(jnp.int32, (16, 128), 1) - Q * lax.broadcasted_iota(jnp.int32, (16, 128), 0)
    scores = jnp.zeros((16, 128), F32)
    for q in range(Q):
        value = jnp.sum(spread[:, q * 128:(q + 1) * 128], axis=1, keepdims=True)
        scores = jnp.where(column == q, value, scores)
    fa[line] = jnp.sum(scores, axis=0, keepdims=True)
    early = list(sends)
    sends.clear()
    send("f line", all_to(fa, line, 2, line_peer))
    late = list(sends)
    sends[:] = early
    drain()
    arrive("f line")
    fb[chip] = jnp.sum(fa[...], axis=0)
    send("f plane", all_to(fb, chip, 3, plane_peer))
    arrive("f plane")
    whole = jnp.broadcast_to(jnp.sum(fb[...], axis=0), (16, 128))
    place = lax.broadcasted_iota(jnp.int32, (16, Q), 1)
    result = jnp.zeros((16, Q), F32)
    for q in range(Q):
        value = jnp.sum(jnp.where(column == q, whole, 0.0), axis=1, keepdims=True)
        result = jnp.where(place == q, value, result)
    out[...] = result
    sends.extend(late)
    finish()


def local(*args):
    dma = pltpu.SemaphoreType.DMA
    vm = pltpu.VMEM
    return pl.pallas_call(
        kernel,
        out_shape=jax.ShapeDtypeStruct((16, Q), F32),
        in_specs=[pl.BlockSpec(memory_space=pl.ANY)] * 7 + [pl.BlockSpec(memory_space=pltpu.SMEM)] * 2,
        out_specs=pl.BlockSpec(memory_space=pltpu.VMEM),
        scratch_shapes=[
            vm((320, 1792), BF16), vm((320, 256), BF16), vm((GROUPS, 1792, 256), BF16), vm((256, 1024), BF16),
            vm((GROUPS, 128, 1024), BF16),
            vm((2, 256, 896), BF16), vm((2, 2, 64, 512), BF16),
            vm((2, 4, 2, 32, 896), BF16), vm((2, 4, 2, 2, 16, 256), BF16),
            vm((32, 896), BF16), vm((2, 16, 256), BF16),
            vm((256, 896), BF16), vm((2, 64, 512), BF16),
            vm((256, 1024), BF16), vm((64, 1024), F32),
            vm((256, 512), BF16), vm((64, 512), F32),
            vm((16, 64, 128), BF16), vm((16, 16, 128), F32),
            vm((256, 1024), BF16), vm((64, 1024), BF16),
            vm((GROUPS, 128, 1024), F32), vm((GROUPS, 256, 512), F32),
            vm((16, 1, 128), F32), vm((16, 1, 128), F32), vm((16, 1, 128), F32), vm((16, 1, 128), F32),
            dma((5 + GROUPS,)), dma((GROUPS,)),
            dma((2, 2, 5, 2)), dma((2, 2, 5, 2)),
            dma((2, 2, 4, 2)), dma((2, 2, 4, 2)),
            dma((6,)), dma((6,)),
            dma((4, 16)), dma((4, 16)),
            dma((4, 16)), dma((4, 16)),
        ],
        name="influence",
        compiler_params=pltpu.CompilerParams(
            collective_id=0, has_side_effects=True, vmem_limit_bytes=63 << 20
        ),
    )(*args)


def solution(mesh):
    in_specs = (
        P(None, ("tok", "inp")),
        P(None, ("tok", "out")),
        P(None, ("tok", "inp")),
        P(None, ("tok", "out")),
        P(("tok", "inp"), "out"),
        P(("tok", "out"), "inp"),
        P("out", "inp"),
        P(),
        P(),
    )
    return jax.shard_map(local, mesh=mesh, in_specs=in_specs, out_specs=P(), check_vma=False)
```

time: 75.3 us -> 62.8 us (0.83)
  Pallas kernels: 68.2 us -> 61.3 us
  local copies, waits for them, and re-layouts: 6.78 us -> 1.35 us
    pallas_call x1, Pallas kernels: 68.2 us -> 61.3 us  [local(): pl.pallas_call(kernel, out_shape=jax.ShapeDtypeStruct((16, Q), F32), in_s...]
    unnamed x14 -> x0, local copies, waits for them, and re-layouts: 6.13 us -> none
where the time goes in v2:
time: 62.8 us; the launch traced here: 62.6 us
  Pallas kernels  61.3 us (98%)
  local copies, waits for them, and re-layouts  1.35 us (2%)
    pallas_call x1, Pallas kernels, local(): pl.pallas_call(kernel, out_shape=jax.ShapeDtypeStruct((16, Q), F32), in_s...  61.3 us
    pallas_call x1, local copies, waits for them, and re-layouts, local(): pl.pallas_call(kernel, out_shape=jax.ShapeDtypeStruct((16, Q), F32), in_s...  1.35 us

profile of v2, /device:TPU:1, one launch (start us, length us, event | category | flops | bytes accessed | tf_op | source)
XLA Modules:
  0.0 62.6 jit_solution(6700930497309851530)
XLA Ops:
  0.0 61.3 %influence.1 = f32[16,4]{1,0:T(8,128)} custom-call(bf16[256,1792]{1,0:T(8,128)(2,1)} %cg.1, bf16[256,256]{1,0:T(8,128)(2,1)} %ca.1, bf16[64,1792]{1,0:T(8,128)(2,1)} %qg.1, bf16[64,256]{1,0:T(8,128)(2,1)} %qa.1, bf16[1792,1792]{1,0:T(8,128)(2,1)} %eo.1, bf16[256,1024]{1,0:T(8,128)(2,1)} %ei.1, bf16[1792,1024]{1,0:T(8,128)(2,1)} %ev.1, s32[16]{0:T(128)} %dl.1, ...), custom_call_target="tpu_custom_call" | custom-call | tf_op jit(solution)/shard_map/influence/pallas_call | solution.py:422
  61.3 1.3 %copy.10 = f32[16,4]{0,1:T(4,128)} copy(f32[16,4]{1,0:T(8,128)} %influence.1) | data formatting | bytes 512 | tf_op jit(solution)/shard_map/influence/pallas_call | solution.py:422

commit v3 on v2

--- a/solution.py
+++ b/solution.py
@@ -57,41 +57,44 @@
     def each(body):
         lax.fori_loop(1, 16, lambda r, carry: (body(r), carry)[1], 0)
 
-    sends, waits = [], {}
-
-    def single(copy):
-        return lambda do: do(copy)
-
-    def several(copies):
-        def run(do):
-            for copy in copies:
-                do(copy)
-        return run
-
-    def bundle(copies):
-        def run(do):
-            def body(r):
-                for copy in copies(r):
-                    do(copy)
-            each(body)
-        return run
-
-    def send(key, run):
-        run(lambda copy: copy.start())
-        sends.append(run)
-        waits[key] = run
+    waits, sends = {}, {}
+
+    def send(key, start, arrivals, departures):
+        start()
+        waits[key] = arrivals
+        for name, leave in departures.items():
+            sends.setdefault(name, []).append(leave)
 
     def arrive(key):
-        waits.pop(key)(lambda copy: copy.wait_recv())
+        for copy in waits.pop(key):
+            copy.wait_recv()
 
     def drain():
-        while sends:
-            sends.pop()(lambda copy: copy.wait_send())
+        for leaves in sends.values():
+            leaves[0](len(leaves)).wait_send()
+        sends.clear()
 
     def finish():
         for key in list(waits):
             arrive(key)
         drain()
+
+    def sized(ref, ss, rs):
+        return remote(ref, ref, ss, rs, dev(0, 0, 1, 0))
+
+    def post(key, copies):
+        def start():
+            for copy in copies:
+                copy.start()
+        send(key, start, copies, {(key, n): (lambda count, copy=copy: copy) for n, copy in enumerate(copies)})
+
+    def exchange(key, copies, whole):
+        def start():
+            def body(r):
+                for copy in copies(r):
+                    copy.start()
+            each(body)
+        send(key, start, whole, {(key, n): (lambda count, copy=copy: copy) for n, copy in enumerate(whole)})
 
     loads = [
         pltpu.make_async_copy(ca, xa.at[pl.ds(0, 256)], ld.at[0]),
@@ -106,7 +109,7 @@
 
     def ev_load(g):
         row = pl.multiple_of((2 * g + tok) * 128, 128)
-        return pltpu.make_async_copy(ev.at[pl.ds(row, 128)], evb.at[g], evs.at[g])
+        return pltpu.make_async_copy(ev.at[pl.ds(row, 128)], evb.at[g], evs.at[0])
 
     for load in loads:
         load.start()
@@ -165,6 +168,7 @@
     BOTH = slice(None)
 
     def rs_copies(kind, d, s, cs):
+        ss, rs = rs_s.at[kind, d, cs], rs_r.at[kind, d, s - 1, cs]
         first = 1 if cs == d else 2
         dz = 1 if d == 0 else 7
         if s < 4:
@@ -172,16 +176,25 @@
                 src = own_part(kind, BOTH, z + sign(d) * (5 - s), cs)
             else:
                 src = slot(kind, d, s - 1, BOTH, cs)
-            return [remote(src, slot(kind, d, s, BOTH, cs), rs_s.at[kind, d, s - 1, cs],
-                           rs_r.at[kind, d, s - 1, cs], dev(0, 0, 0, dz))]
+            return [remote(src, slot(kind, d, s, BOTH, cs), ss, rs, dev(0, 0, 0, dz))]
         return [
-            remote(slot(kind, d, 3, t, cs), slot(kind, d, 4, j, cs), rs_s.at[kind, d, 3 + j, cs],
-                   rs_r.at[kind, d, 3 + j, cs], dev(2 * j, 0, 0, dz))
+            remote(slot(kind, d, 3, t, cs), slot(kind, d, 4, j, cs), ss, rs, dev(2 * j, 0, 0, dz))
             for j, t in ((1, 1 - tok), (0, tok))
         ]
 
     def rs_send(kind, d, s, cs):
-        send(("rs", kind, d, s, cs), several(rs_copies(kind, d, s, cs)))
+        def start():
+            for copy in rs_copies(kind, d, s, cs):
+                copy.start()
+
+        def leave(count):
+            if kind == 0:
+                return sized(rsq.at[d, pl.ds(0, count), :, cs], rs_s.at[kind, d, cs], rs_r.at[kind, d, 0, cs])
+            return sized(rsc.at[d, pl.ds(0, count), :, :, pl.ds(*SETS[cs])], rs_s.at[kind, d, cs],
+                         rs_r.at[kind, d, 0, cs])
+
+        whole = sized(slot(kind, d, s, BOTH, cs), rs_s.at[kind, d, cs], rs_r.at[kind, d, s - 1, cs])
+        send(("rs", kind, d, s, cs), start, [whole], {("rs", kind, d, cs): leave})
 
     def rs_step(kind, s):
         for n in range(2 if s > 1 else 1):
@@ -201,19 +214,19 @@
         rs_send(kind, 1, 2, 0)
     other = pl.ds(pl.multiple_of((1 - c) * 512, 512), 512)
     mine = pl.ds(pl.multiple_of(c * 512, 512), 512)
-    send("core 1", several([
+    post("core 1", [
         remote(apc.at[:, other], rac, co_s.at[0], co_r.at[0], dev(0, 0, 1, 0)),
         remote(apq.at[:, other], raq, co_s.at[1], co_r.at[1], dev(0, 0, 1, 0)),
-    ]))
+    ])
     for g in range(4, 7):
         rotate(g)
     for kind in range(2):
         rs_send(kind, 1, 1, 1)
         rs_send(kind, 0, 2, 1)
-    send("own", several([
+    post("own", [
         remote(gpq.at[1 - tok, :, q_rows(z), q_cols(z)], oxq, co_s.at[4], co_r.at[4], dev(2, 0, 0, 0)),
         remote(gpc.at[1 - tok, c_rows(z)], oxc, co_s.at[5], co_r.at[5], dev(2, 0, 0, 0)),
-    ]))
+    ])
 
     arrive("core 1")
     rac[...] = (rac[...].astype(F32) + apc[:, mine].astype(F32)).astype(BF16)
@@ -225,12 +238,15 @@
         cols = pl.ds(pl.multiple_of(lax.rem(y + dy, 4) * 128, 128), 128)
         return (
             remote(rac.at[pl.ds(pl.multiple_of(nx * 64, 64), 64), cols], rdc.at[chip],
-                   pr_s.at[0, r], pr_r.at[0, r], plane_peer(r)),
+                   pr_s.at[0], pr_r.at[0], plane_peer(r)),
             remote(raq.at[pl.ds(pl.multiple_of(nx * 16, 16), 16), cols], rdq.at[chip],
-                   pr_s.at[1, r], pr_r.at[1, r], plane_peer(r)),
-        )
-
-    send("scatter", bundle(a_scatter))
+                   pr_s.at[1], pr_r.at[1], plane_peer(r)),
+        )
+
+    exchange("scatter", a_scatter, [
+        sized(rdc.at[pl.ds(0, 15)], pr_s.at[0], pr_r.at[0]),
+        sized(rdq.at[pl.ds(0, 15)], pr_s.at[1], pr_r.at[1]),
+    ])
     own_rows_c = pl.ds(pl.multiple_of(x * 64, 64), 64)
     own_rows_q = pl.ds(pl.multiple_of(x * 16, 16), 16)
     own_cols = pl.ds(pl.multiple_of(y * 128, 128), 128)
@@ -241,26 +257,29 @@
         rs_step(kind, 1)
 
     total = jnp.zeros((8, 128), F32)
+    pltpu.make_async_copy(evb, evb, evs.at[0]).wait()
     for g in range(GROUPS):
-        ev_load(g).wait()
         for cb in range(8):
             vals = evb[g, :, cb * 128:(cb + 1) * 128].astype(F32)
             total = total + jnp.sum(vals.reshape(16, 8, 128), axis=0)
 
-    def all_to(buf, place, kind, peer):
+    def all_to(key, buf, place, kind, peer):
         def body(r):
-            return [remote(buf.at[place], buf.at[place], st_s.at[kind, r], st_r.at[kind, r], peer(r))]
-        return bundle(body)
+            return [remote(buf.at[place], buf.at[place], st_s.at[kind], st_r.at[kind], peer(r))]
+        exchange(key, body, [sized(buf.at[pl.ds(0, 15)], st_s.at[kind], st_r.at[kind])])
 
     ea[line] = jnp.sum(total, axis=0, keepdims=True)
-    send("e line", all_to(ea, line, 0, line_peer))
+    all_to("e line", ea, line, 0, line_peer)
 
     for kind in range(2):
         rs_step(kind, 2)
 
     arrive("e line")
     eb[chip] = jnp.sum(ea[...], axis=0)
-    send("e plane", all_to(eb, chip, 1, plane_peer))
+    all_to("e plane", eb, chip, 1, plane_peer)
+
+    for kind in range(2):
+        rs_step(kind, 3)
 
     arrive("scatter")
     piece_cols = pl.ds(pl.multiple_of(c * 512 + y * 128, 128), 128)
@@ -270,15 +289,15 @@
     def a_gather(r):
         return (
             remote(afc.at[own_rows_c, piece_cols], afc.at[own_rows_c, piece_cols],
-                   pr_s.at[2, r], pr_r.at[2, r], plane_peer(r)),
+                   pr_s.at[2], pr_r.at[2], plane_peer(r)),
             remote(afq.at[own_rows_q, piece_cols], afq.at[own_rows_q, piece_cols],
-                   pr_s.at[3, r], pr_r.at[3, r], plane_peer(r)),
-        )
-
-    send("gather", bundle(a_gather))
-
-    for kind in range(2):
-        rs_step(kind, 3)
+                   pr_s.at[3], pr_r.at[3], plane_peer(r)),
+        )
+
+    exchange("gather", a_gather, [
+        sized(afc.at[pl.ds(0, 240), pl.ds(0, 512)], pr_s.at[2], pr_r.at[2]),
+        sized(afq.at[pl.ds(0, 48), pl.ds(0, 640)], pr_s.at[3], pr_r.at[3]),
+    ])
 
     arrive("own")
 
@@ -289,11 +308,20 @@
 
     def ag_copy(kind, d, s, cs):
         part = full_part(kind, z - sign(d) * (s - 1), cs)
-        return remote(part, part, ag_s.at[kind, d, s - 1, cs], ag_r.at[kind, d, s - 1, cs],
+        return remote(part, part, ag_s.at[kind, d, cs], ag_r.at[kind, d, s - 1, cs],
                       dev(0, 0, 0, 1 if d == 0 else 7))
 
     def ag_send(kind, d, s, cs):
-        send(("ag", kind, d, s, cs), single(ag_copy(kind, d, s, cs)))
+        copy = ag_copy(kind, d, s, cs)
+
+        def leave(count):
+            if kind == 0:
+                ref = gfq.at[cs, pl.ds(0, 16 * count), pl.ds(0, 256)]
+            else:
+                ref = gfc.at[pl.ds(0, 32 * count), pl.ds(*SETS[cs])]
+            return sized(ref, ag_s.at[kind, d, cs], ag_r.at[kind, d, 0, cs])
+
+        send(("ag", kind, d, s, cs), copy.start, [copy], {("ag", kind, d, cs): leave})
 
     def owner_sum(kind):
         for cs in range(2):
@@ -331,10 +359,10 @@
 
     ag_step(0, 1)
     arrive("gather")
-    send("core 2", several([
+    post("core 2", [
         remote(afc.at[:, mine], afc.at[:, mine], co_s.at[2], co_r.at[2], dev(0, 0, 1, 0)),
         remote(afq.at[:, mine], afq.at[:, mine], co_s.at[3], co_r.at[3], dev(0, 0, 1, 0)),
-    ]))
+    ])
     ag_step(1, 1)
 
     ids = jnp.zeros((1, 64), jnp.int32)
@@ -395,15 +423,17 @@
         value = jnp.sum(spread[:, q * 128:(q + 1) * 128], axis=1, keepdims=True)
         scores = jnp.where(column == q, value, scores)
     fa[line] = jnp.sum(scores, axis=0, keepdims=True)
-    early = list(sends)
+    early = dict(sends)
     sends.clear()
-    send("f line", all_to(fa, line, 2, line_peer))
-    late = list(sends)
-    sends[:] = early
+    all_to("f line", fa, line, 2, line_peer)
+    late = dict(sends)
+    sends.clear()
+    sends.update(early)
     drain()
+    sends.update(late)
     arrive("f line")
     fb[chip] = jnp.sum(fa[...], axis=0)
-    send("f plane", all_to(fb, chip, 3, plane_peer))
+    all_to("f plane", fb, chip, 3, plane_peer)
     arrive("f plane")
     whole = jnp.broadcast_to(jnp.sum(fb[...], axis=0), (16, 128))
     place = lax.broadcasted_iota(jnp.int32, (16, Q), 1)
@@ -412,7 +442,6 @@
         value = jnp.sum(jnp.where(column == q, whole, 0.0), axis=1, keepdims=True)
         result = jnp.where(place == q, value, result)
     out[...] = result
-    sends.extend(late)
     finish()
 
 
@@ -437,12 +466,12 @@
             vm((256, 1024), BF16), vm((64, 1024), BF16),
             vm((GROUPS, 128, 1024), F32), vm((GROUPS, 256, 512), F32),
             vm((16, 1, 128), F32), vm((16, 1, 128), F32), vm((16, 1, 128), F32), vm((16, 1, 128), F32),
-            dma((5 + GROUPS,)), dma((GROUPS,)),
-            dma((2, 2, 5, 2)), dma((2, 2, 5, 2)),
-            dma((2, 2, 4, 2)), dma((2, 2, 4, 2)),
+            dma((5 + GROUPS,)), dma((1,)),
+            dma((2, 2, 2)), dma((2, 2, 4, 2)),
+            dma((2, 2, 2)), dma((2, 2, 4, 2)),
             dma((6,)), dma((6,)),
-            dma((4, 16)), dma((4, 16)),
-            dma((4, 16)), dma((4, 16)),
+            dma((4,)), dma((4,)),
+            dma((4,)), dma((4,)),
         ],
         name="influence",
         compiler_params=pltpu.CompilerParams(

time: 62.8 us -> 60.4 us (0.962)
  Pallas kernels: 61.3 us -> 58.9 us
    pallas_call x1, Pallas kernels: 61.3 us -> 58.9 us  [local(): pl.pallas_call(kernel, out_shape=jax.ShapeDtypeStruct((16, Q), F32), in_s...]
where the time goes in v3:
time: 60.4 us; the launch traced here: 60.3 us
  Pallas kernels  58.9 us (98%)
  local copies, waits for them, and re-layouts  1.35 us (2%)
    pallas_call x1, Pallas kernels, local(): pl.pallas_call(kernel, out_shape=jax.ShapeDtypeStruct((16, Q), F32), in_s...  58.9 us
    pallas_call x1, local copies, waits for them, and re-layouts, local(): pl.pallas_call(kernel, out_shape=jax.ShapeDtypeStruct((16, Q), F32), in_s...  1.35 us

profile of v3, /device:TPU:1, one launch (start us, length us, event | category | flops | bytes accessed | tf_op | source)
XLA Modules:
  0.0 60.3 jit_solution(13406535984891556244)
XLA Ops:
  0.0 58.9 %influence.1 = f32[16,4]{1,0:T(8,128)} custom-call(bf16[256,1792]{1,0:T(8,128)(2,1)} %cg.1, bf16[256,256]{1,0:T(8,128)(2,1)} %ca.1, bf16[64,1792]{1,0:T(8,128)(2,1)} %qg.1, bf16[64,256]{1,0:T(8,128)(2,1)} %qa.1, bf16[1792,1792]{1,0:T(8,128)(2,1)} %eo.1, bf16[256,1024]{1,0:T(8,128)(2,1)} %ei.1, bf16[1792,1024]{1,0:T(8,128)(2,1)} %ev.1, s32[16]{0:T(128)} %dl.1, ...), custom_call_target="tpu_custom_call" | custom-call | tf_op jit(solution)/shard_map/influence/pallas_call | solution.py:451
  58.9 1.3 %copy.10 = f32[16,4]{0,1:T(4,128)} copy(f32[16,4]{1,0:T(8,128)} %influence.1) | data formatting | bytes 512 | tf_op jit(solution)/shard_map/influence/pallas_call | solution.py:451

commit v4 on v3

v4 whole, which is shorter than its diff:
```python
import jax
import jax.numpy as jnp
from jax import lax
from jax.experimental import pallas as pl
from jax.experimental.pallas import tpu as pltpu
from jax.sharding import PartitionSpec as P

D = 8192
FF = 28672
Q = 4
MESH = pl.DeviceIdType.MESH
F32 = jnp.float32
BF16 = jnp.bfloat16
GROUPS = 7
SETS = ((0, 256), (256, 256), (512, 256), (768, 128))
ENDS = ((0, 512), (512, 384))


def kernel(
    cg, ca, qg, qa, eo, ei, ev, dl, qi, out,
    xg, xa, eob, eib, evb, gpc, gpq, rsc, rsq, oxc, oxq, gfc, gfq,
    apk, rap, rda, afa, inv, mm, ea, eb, fa, fb,
    ld, evs, rq_s, rq_r, rc_s, rc_r, ag_s, ag_r, co_s, co_r, pr_s, pr_r, st_s, st_r,
):
    tok, o, z = lax.axis_index("tok"), lax.axis_index("out"), lax.axis_index("inp")
    x = tok * 2 + o // 8
    y = lax.rem(o // 2, 4)
    c = lax.rem(o, 2)
    chip = x * 4 + y
    line = c * 8 + z

    def dev(dx, dy, dc, dz):
        nx = lax.rem(x + dx, 4)
        ny = lax.rem(y + dy, 4)
        nc = lax.rem(c + dc, 2)
        return (nx // 2, lax.rem(nx, 2) * 8 + ny * 2 + nc, lax.rem(z + dz, 8))

    def remote(src, dst, ss, rs, where):
        return pltpu.make_async_remote_copy(
            src_ref=src, dst_ref=dst, send_sem=ss, recv_sem=rs, device_id=where, device_id_type=MESH
        )

    def line_peer(r):
        n = r - 1 + r // 15
        j = n // 2
        odd = lax.rem(j, 2)
        dz = 4 + odd * ((j + 1) // 2) + (1 - odd) * (8 - j // 2)
        return dev(0, 0, lax.rem(n, 2), dz)

    def plane_shift(r):
        n = r - 1 + r // 11
        return lax.rem(2 + n // 4, 4), lax.rem(2 + lax.rem(n, 4), 4)

    def plane_peer(r):
        dx, dy = plane_shift(r)
        return dev(dx, dy, 0, 0)

    def each(body):
        lax.fori_loop(1, 16, lambda r, carry: (body(r), carry)[1], 0)

    waits, sends = {}, {}

    def send(key, start, arrivals, departures):
        start()
        waits[key] = arrivals
        for name, leave in departures.items():
            sends.setdefault(name, []).append(leave)

    def arrive(key):
        for copy in waits.pop(key):
            copy.wait_recv()

    def drain():
        for leaves in sends.values():
            leaves[0](len(leaves)).wait_send()
        sends.clear()

    def finish():
        for key in list(waits):
            arrive(key)
        drain()

    def sized(ref, ss, rs):
        return remote(ref, ref, ss, rs, dev(0, 0, 1, 0))

    def post(key, copies):
        def start():
            for copy in copies:
                copy.start()
        send(key, start, copies, {(key, n): (lambda count, copy=copy: copy) for n, copy in enumerate(copies)})

    def exchange(key, copies, whole):
        def start():
            def body(r):
                for copy in copies(r):
                    copy.start()
            each(body)
        send(key, start, whole, {(key, n): (lambda count, copy=copy: copy) for n, copy in enumerate(whole)})

    loads = [
        pltpu.make_async_copy(ca, xa.at[pl.ds(0, 256)], ld.at[0]),
        pltpu.make_async_copy(qa, xa.at[pl.ds(256, 64)], ld.at[1]),
        pltpu.make_async_copy(ei, eib, ld.at[2]),
        pltpu.make_async_copy(cg, xg.at[pl.ds(0, 256)], ld.at[3]),
        pltpu.make_async_copy(qg, xg.at[pl.ds(256, 64)], ld.at[4]),
    ]

    def eo_load(g):
        return pltpu.make_async_copy(eo.at[:, pl.ds(pl.multiple_of(g * 256, 256), 256)], eob.at[g], ld.at[5 + g])

    def ev_load(g):
        row = pl.multiple_of((2 * g + tok) * 128, 128)
        return pltpu.make_async_copy(ev.at[pl.ds(row, 128)], evb.at[g], evs.at[0])

    for load in loads:
        load.start()
    for g in range(GROUPS):
        eo_load(g).start()

    barrier = pltpu.get_barrier_semaphore()

    def greet(r):
        pl.semaphore_signal(barrier, inc=1, device_id=line_peer(r), device_id_type=MESH)
        pl.semaphore_signal(barrier, inc=1, device_id=plane_peer(r), device_id_type=MESH)

    each(greet)
    for g in range(GROUPS):
        ev_load(g).start()

    for load in loads[:3]:
        load.wait()
    apart = jnp.dot(xa[...], eib[...], preferred_element_type=F32)
    for i in range(4):
        apk[i, :64] = apart[i * 64:(i + 1) * 64]
        apk[i, 64:] = apart[256 + i * 16:256 + (i + 1) * 16]

    for load in loads[3:]:
        load.wait()
    gpq[:, 1, :, 384:] = jnp.zeros((2, 64, 128), F32)

    def rotate(g):
        eo_load(g).wait()
        part = jnp.dot(xg[...], eob[g], preferred_element_type=F32)
        for t in range(2):
            gpc[t, :, g * 128:(g + 1) * 128] = part[:256, t * 128:(t + 1) * 128].astype(BF16)
            gpq[t, g // 4, :, (g % 4) * 128:(g % 4 + 1) * 128] = part[256:, t * 128:(t + 1) * 128]

    def c_rows(owner):
        return pl.ds(pl.multiple_of(lax.rem(owner + 16, 8) * 32, 32), 32)

    def q_rows(owner):
        return pl.ds(pl.multiple_of(lax.rem(owner + 16, 8) // 2 * 16, 16), 16)

    def q_cols(owner):
        return pl.ds(pl.multiple_of(lax.rem(owner + 16, 2) * 256, 256), 256)

    def own_q(t, owner):
        return gpq.at[t, :, q_rows(owner), q_cols(owner)]

    def own_c(t, owner, cs):
        return gpc.at[t, c_rows(owner), pl.ds(*SETS[cs])]

    def sign(d):
        return 1 if d == 0 else -1

    BOTH = slice(None)

    def rs_q(d, s):
        ss, rs = rq_s.at[d], rq_r.at[d, s - 1]
        dz = 1 if d == 0 else 7
        if s < 4:
            src = own_q(BOTH, z + sign(d) * (5 - s)) if s == d + 1 else rsq.at[d, s - 2]
            copies = [remote(src, rsq.at[d, s - 1], ss, rs, dev(0, 0, 0, dz))]
        else:
            copies = [remote(rsq.at[d, 2, t], rsq.at[d, 3, j], ss, rs, dev(2 * j, 0, 0, dz))
                      for j, t in ((1, 1 - tok), (0, tok))]

        def start():
            for copy in copies:
                copy.start()

        send(("rq", d, s), start, [sized(rsq.at[d, s - 1], ss, rs)],
             {("rq", d): lambda count: sized(rsq.at[d, pl.ds(0, count)], ss, rs)})

    def slot(d, s, t, cs):
        return rsc.at[d, s - 1, t, :, pl.ds(*SETS[cs])]

    def rs_c(d, s, cs):
        ss, rs = rc_s.at[d, cs], rc_r.at[d, s - 1, cs]
        dz = 1 if d == 0 else 7
        first = 1 if cs % 2 == d else 2
        if s < 4:
            src = own_c(BOTH, z + sign(d) * (5 - s), cs) if s == first else slot(d, s - 1, BOTH, cs)
            copies = [remote(src, slot(d, s, BOTH, cs), ss, rs, dev(0, 0, 0, dz))]
        else:
            copies = [remote(slot(d, 3, t, cs), slot(d, 4, j, cs), ss, rs, dev(2 * j, 0, 0, dz))
                      for j, t in ((1, 1 - tok), (0, tok))]

        def start():
            for copy in copies:
                copy.start()

        send(("rc", d, s, cs), start, [sized(slot(d, s, BOTH, cs), ss, rs)],
             {("rc", d, cs): lambda count: sized(rsc.at[d, pl.ds(0, count), :, :, pl.ds(*SETS[cs])], ss, rs)})

    def add_to(held, own):
        held[...] = (held[...].astype(F32) + own[...].astype(F32)).astype(held.dtype)

    def rs_step(s):
        for d in range(2 if s > 1 else 1):
            arrive(("rq", d, s))
            add_to(rsq.at[d, s - 1], own_q(BOTH, z + sign(d) * (4 - s)))
            rs_q(d, s + 1)
        for cs in range(4):
            for d in ((cs % 2, 1 - cs % 2) if s > 1 else (cs % 2,)):
                arrive(("rc", d, s, cs))
                add_to(slot(d, s, BOTH, cs), own_c(BOTH, z + sign(d) * (4 - s), cs))
                rs_c(d, s + 1, cs)

    for g in range(4):
        rotate(g)
    pl.semaphore_wait(barrier, 30)
    for cs in range(2):
        rs_c(cs, 1, cs)
    for cs in range(2):
        rs_c(1 - cs, 2, cs)
    other = pl.ds(pl.multiple_of((1 - c) * 512, 512), 512)
    mine = pl.ds(pl.multiple_of(c * 512, 512), 512)
    post("core 1", [remote(apk.at[:, :, other], rap, co_s.at[0], co_r.at[0], dev(0, 0, 1, 0))])
    for g in range(4, 7):
        rotate(g)
    rs_q(0, 1)
    rs_q(1, 2)
    for cs in range(2, 4):
        rs_c(cs - 2, 1, cs)
    for cs in range(2, 4):
        rs_c(3 - cs, 2, cs)
    post("own", [
        remote(own_q(1 - tok, z), oxq, co_s.at[2], co_r.at[2], dev(2, 0, 0, 0)),
        remote(gpc.at[1 - tok, c_rows(z)], oxc, co_s.at[3], co_r.at[3], dev(2, 0, 0, 0)),
    ])

    arrive("core 1")
    rap[...] = rap[...] + apk[:, :, mine]

    def a_scatter(r):
        dx, dy = plane_shift(r)
        cols = pl.ds(pl.multiple_of(lax.rem(y + dy, 4) * 128, 128), 128)
        return [remote(rap.at[lax.rem(x + dx, 4), :, cols], rda.at[chip], pr_s.at[0], pr_r.at[0], plane_peer(r))]

    exchange("scatter", a_scatter, [sized(rda.at[pl.ds(0, 15)], pr_s.at[0], pr_r.at[0])])
    rda[chip] = rap[x, :, pl.ds(pl.multiple_of(y * 128, 128), 128)]

    rs_step(1)

    total = jnp.zeros((8, 128), F32)
    pltpu.make_async_copy(evb, evb, evs.at[0]).wait()
    for g in range(GROUPS):
        for cb in range(8):
            vals = evb[g, :, cb * 128:(cb + 1) * 128].astype(F32)
            total = total + jnp.sum(vals.reshape(16, 8, 128), axis=0)

    def all_to(key, buf, place, kind, peer):
        def body(r):
            return [remote(buf.at[place], buf.at[place], st_s.at[kind], st_r.at[kind], peer(r))]
        exchange(key, body, [sized(buf.at[pl.ds(0, 15)], st_s.at[kind], st_r.at[kind])])

    ea[line] = jnp.sum(total, axis=0, keepdims=True)
    all_to("e line", ea, line, 0, line_peer)

    rs_step(2)

    arrive("e line")
    eb[chip] = jnp.sum(ea[...], axis=0)
    all_to("e plane", eb, chip, 1, plane_peer)

    rs_step(3)

    arrive("scatter")
    piece_cols = pl.ds(pl.multiple_of(c * 512 + y * 128, 128), 128)
    afa[x, :, piece_cols] = jnp.sum(rda[...], axis=0).astype(BF16)

    def a_gather(r):
        ref = afa.at[x, :, piece_cols]
        return [remote(ref, ref, pr_s.at[1], pr_r.at[1], plane_peer(r))]

    exchange("gather", a_gather, [sized(afa.at[pl.ds(0, 3), :, pl.ds(0, 640)], pr_s.at[1], pr_r.at[1])])

    arrive("own")

    for d in range(2):
        arrive(("rq", d, 4))
    value = own_q(tok, z)[...].astype(F32) + oxq[...].astype(F32)
    for d in range(2):
        for j in range(2):
            value = value + rsq[d, 3, j].astype(F32)
    gfq[z] = value.astype(BF16)

    def q_gather_start():
        for dz in (4, 3, 5, 2, 6, 1, 7):
            remote(gfq.at[z], gfq.at[z], pr_s.at[2], pr_r.at[2], dev(0, 0, 0, dz)).start()

    q_whole = sized(gfq.at[pl.ds(0, 7)], pr_s.at[2], pr_r.at[2])
    send("q gather", q_gather_start, [q_whole], {"q gather": lambda count: q_whole})

    for cs in range(4):
        for d in range(2):
            arrive(("rc", d, 4, cs))
        value = own_c(tok, z, cs)[...].astype(F32) + oxc[:, pl.ds(*SETS[cs])].astype(F32)
        for d in range(2):
            for j in range(2):
                value = value + slot(d, 4, j, cs)[...].astype(F32)
        gfc[c_rows(z), pl.ds(*SETS[cs])] = value.astype(BF16)

    def ag_post(key, n, owner, cols, dz):
        ref = gfc.at[c_rows(owner), cols]
        post(key, [remote(ref, ref, ag_s.at[n], ag_r.at[n], dev(0, 0, 0, dz))])

    for cs in range(2):
        for d in range(2):
            ag_post(("second", d, cs), d * 2 + cs, z, pl.ds(*ENDS[cs]), 2 if d == 0 else 6)
    for d in range(2):
        ag_post(("next", d), 4 + d, z, pl.ds(0, 896), 1 if d == 0 else 7)

    arrive("e plane")
    eigen_sum = jnp.sum(jnp.sum(eb[...], axis=0))
    damping = 0.1 * eigen_sum / (FF * D)

    def invert(g, carry):
        inv[g] = 1.0 / (evb[g].astype(F32) + damping)
        return carry

    lax.fori_loop(0, GROUPS, invert, 0)

    for cs in range(2):
        for d in range(2):
            arrive(("second", d, cs))
            owner = z - 2 * sign(d)
            if cs == d:
                ag_post(("fourth", d), 6 + d, owner, pl.ds(*ENDS[cs]), 2 if d == 0 else 6)
            ag_post(("third", d, cs), 8 + d * 2 + cs, owner, pl.ds(*ENDS[cs]), 1 if d == 0 else 7)
    arrive("gather")
    post("core 2", [remote(afa.at[:, :, mine], afa.at[:, :, mine], co_s.at[1], co_r.at[1], dev(0, 0, 1, 0))])

    ids = jnp.zeros((1, 64), jnp.int32)
    lane = lax.broadcasted_iota(jnp.int32, (1, 64), 1)
    for s in range(64):
        ids = jnp.where(lane == s, qi[s], ids)
    doc = lax.broadcasted_iota(jnp.int32, (16, 256), 0)
    position = lax.broadcasted_iota(jnp.int32, (16, 256), 1)
    first = jnp.zeros((16, 256), jnp.int32)
    last = jnp.zeros((16, 256), jnp.int32)
    start = jnp.int32(0)
    for n in range(16):
        stop = start + dl[n]
        first = jnp.where(doc == n, start, first)
        last = jnp.where(doc == n, stop, last)
        start = stop
    member = ((position >= first) & (position < last)).astype(F32)

    arrive("q gather")
    arrive("core 2")

    def contract(g, carry):
        cols = pl.ds(pl.multiple_of(lax.rem(g, 2) * 128, 128), 128)
        half = lax.rem(g, 4) // 2
        rows = jnp.concatenate([gfq[2 * i + half, g // 4, :, cols].astype(F32) for i in range(4)], axis=0)
        turned = rows.T
        stacked = jnp.concatenate(
            [jnp.where(ids == q, turned, 0.0).astype(BF16) for q in range(Q)], axis=0
        )
        query_acts = jnp.concatenate([afa[i, 64:] for i in range(4)], axis=0)
        cand_acts = jnp.concatenate([afa[i, :64] for i in range(4)], axis=0)
        outer = jnp.dot(stacked, query_acts, preferred_element_type=F32)
        scale = inv[g]
        precond = jnp.concatenate(
            [(scale * outer[q * 128:(q + 1) * 128]).astype(BF16) for q in range(Q)], axis=0
        )
        mm[g] = lax.dot_general(
            cand_acts, precond, (((1,), (1,)), ((), ())), preferred_element_type=F32
        )
        return carry

    lax.fori_loop(0, GROUPS, contract, 0)
    for d in range(2):
        arrive(("next", d))
        arrive(("fourth", d))
        for cs in range(2):
            arrive(("third", d, cs))

    columns = []
    for q in range(Q):
        acc = jnp.zeros((256, 128), F32)
        for g in range(GROUPS):
            acc = acc + gfc[:, g * 128:(g + 1) * 128].astype(F32) * mm[g, :, q * 128:(q + 1) * 128]
        columns.append(acc)
    spread = jnp.dot(
        member, jnp.concatenate(columns, axis=1), precision=lax.Precision.HIGHEST, preferred_element_type=F32
    )
    column = lax.broadcasted_iota(jnp.int32, (16, 128), 1) - Q * lax.broadcasted_iota(jnp.int32, (16, 128), 0)
    scores = jnp.zeros((16, 128), F32)
    for q in range(Q):
        value = jnp.sum(spread[:, q * 128:(q + 1) * 128], axis=1, keepdims=True)
        scores = jnp.where(column == q, value, scores)
    fa[line] = jnp.sum(scores, axis=0, keepdims=True)
    early = dict(sends)
    sends.clear()
    all_to("f line", fa, line, 2, line_peer)
    late = dict(sends)
    sends.clear()
    sends.update(early)
    drain()
    sends.update(late)
    arrive("f line")
    fb[chip] = jnp.sum(fa[...], axis=0)
    all_to("f plane", fb, chip, 3, plane_peer)
    arrive("f plane")
    whole = jnp.broadcast_to(jnp.sum(fb[...], axis=0), (16, 128))
    place = lax.broadcasted_iota(jnp.int32, (16, Q), 1)
    result = jnp.zeros((16, Q), F32)
    for q in range(Q):
        value = jnp.sum(jnp.where(column == q, whole, 0.0), axis=1, keepdims=True)
        result = jnp.where(place == q, value, result)
    out[...] = result
    finish()


def local(*args):
    dma = pltpu.SemaphoreType.DMA
    vm = pltpu.VMEM
    return pl.pallas_call(
        kernel,
        out_shape=jax.ShapeDtypeStruct((16, Q), F32),
        in_specs=[pl.BlockSpec(memory_space=pl.ANY)] * 7 + [pl.BlockSpec(memory_space=pltpu.SMEM)] * 2,
        out_specs=pl.BlockSpec(memory_space=pltpu.VMEM),
        scratch_shapes=[
            vm((320, 1792), BF16), vm((320, 256), BF16), vm((GROUPS, 1792, 256), BF16), vm((256, 1024), BF16),
            vm((GROUPS, 128, 1024), BF16),
            vm((2, 256, 896), BF16), vm((2, 2, 64, 512), F32),
            vm((2, 4, 2, 32, 896), BF16), vm((2, 4, 2, 2, 16, 256), F32),
            vm((32, 896), BF16), vm((2, 16, 256), F32),
            vm((256, 896), BF16), vm((8, 2, 16, 256), BF16),
            vm((4, 80, 1024), F32), vm((4, 80, 512), F32), vm((16, 80, 128), F32), vm((4, 80, 1024), BF16),
            vm((GROUPS, 128, 1024), F32), vm((GROUPS, 256, 512), F32),
            vm((16, 1, 128), F32), vm((16, 1, 128), F32), vm((16, 1, 128), F32), vm((16, 1, 128), F32),
            dma((5 + GROUPS,)), dma((1,)),
            dma((2,)), dma((2, 4)),
            dma((2, 4)), dma((2, 4, 4)),
            dma((12,)), dma((12,)),
            dma((4,)), dma((4,)),
            dma((3,)), dma((3,)),
            dma((4,)), dma((4,)),
        ],
        name="influence",
        compiler_params=pltpu.CompilerParams(
            collective_id=0, has_side_effects=True, vmem_limit_bytes=63 << 20
        ),
    )(*args)


def solution(mesh):
    in_specs = (
        P(None, ("tok", "inp")),
        P(None, ("tok", "out")),
        P(None, ("tok", "inp")),
        P(None, ("tok", "out")),
        P(("tok", "inp"), "out"),
        P(("tok", "out"), "inp"),
        P("out", "inp"),
        P(),
        P(),
    )
    return jax.shard_map(local, mesh=mesh, in_specs=in_specs, out_specs=P(), check_vma=False)
```

time: 60.4 us -> 58.6 us (0.970)
  Pallas kernels: 58.9 us -> 57.1 us
    pallas_call x1, Pallas kernels: 58.9 us -> 57.1 us  [local(): pl.pallas_call(kernel, out_shape=jax.ShapeDtypeStruct((16, Q), F32), in_s...]
where the time goes in v4:
time: 58.6 us; the launch traced here: 58.4 us
  Pallas kernels  57.1 us (97%)
  local copies, waits for them, and re-layouts  1.35 us (2%)
    pallas_call x1, Pallas kernels, local(): pl.pallas_call(kernel, out_shape=jax.ShapeDtypeStruct((16, Q), F32), in_s...  57.1 us
    pallas_call x1, local copies, waits for them, and re-layouts, local(): pl.pallas_call(kernel, out_shape=jax.ShapeDtypeStruct((16, Q), F32), in_s...  1.35 us

profile of v4, /device:TPU:1, one launch (start us, length us, event | category | flops | bytes accessed | tf_op | source)
XLA Modules:
  0.0 58.4 jit_solution(17541770113107089139)
XLA Ops:
  0.0 57.1 %influence.1 = f32[16,4]{1,0:T(8,128)} custom-call(bf16[256,1792]{1,0:T(8,128)(2,1)} %cg.1, bf16[256,256]{1,0:T(8,128)(2,1)} %ca.1, bf16[64,1792]{1,0:T(8,128)(2,1)} %qg.1, bf16[64,256]{1,0:T(8,128)(2,1)} %qa.1, bf16[1792,1792]{1,0:T(8,128)(2,1)} %eo.1, bf16[256,1024]{1,0:T(8,128)(2,1)} %ei.1, bf16[1792,1024]{1,0:T(8,128)(2,1)} %ev.1, s32[16]{0:T(128)} %dl.1, ...), custom_call_target="tpu_custom_call" | custom-call | tf_op jit(solution)/shard_map/influence/pallas_call | solution.py:431
  57.1 1.3 %copy.10 = f32[16,4]{0,1:T(4,128)} copy(f32[16,4]{1,0:T(8,128)} %influence.1) | data formatting | bytes 512 | tf_op jit(solution)/shard_map/influence/pallas_call | solution.py:431

commit v5 on v4

--- a/solution.py
+++ b/solution.py
@@ -89,8 +89,14 @@
                 copy.start()
         send(key, start, copies, {(key, n): (lambda count, copy=copy: copy) for n, copy in enumerate(copies)})
 
-    def exchange(key, copies, whole):
+    def exchange(key, copies, whole, unrolled=False):
         def start():
+            if unrolled:
+                for r in range(1, 16):
+                    for copy in copies(r):
+                        copy.start()
+                return
+
             def body(r):
                 for copy in copies(r):
                     copy.start()
@@ -123,7 +129,8 @@
         pl.semaphore_signal(barrier, inc=1, device_id=line_peer(r), device_id_type=MESH)
         pl.semaphore_signal(barrier, inc=1, device_id=plane_peer(r), device_id_type=MESH)
 
-    each(greet)
+    for r in range(1, 16):
+        greet(r)
     for g in range(GROUPS):
         ev_load(g).start()
 
@@ -260,10 +267,10 @@
             vals = evb[g, :, cb * 128:(cb + 1) * 128].astype(F32)
             total = total + jnp.sum(vals.reshape(16, 8, 128), axis=0)
 
-    def all_to(key, buf, place, kind, peer):
+    def all_to(key, buf, place, kind, peer, unrolled=False):
         def body(r):
             return [remote(buf.at[place], buf.at[place], st_s.at[kind], st_r.at[kind], peer(r))]
-        exchange(key, body, [sized(buf.at[pl.ds(0, 15)], st_s.at[kind], st_r.at[kind])])
+        exchange(key, body, [sized(buf.at[pl.ds(0, 15)], st_s.at[kind], st_r.at[kind])], unrolled)
 
     ea[line] = jnp.sum(total, axis=0, keepdims=True)
     all_to("e line", ea, line, 0, line_peer)
@@ -302,6 +309,10 @@
 
     q_whole = sized(gfq.at[pl.ds(0, 7)], pr_s.at[2], pr_r.at[2])
     send("q gather", q_gather_start, [q_whole], {"q gather": lambda count: q_whole})
+
+    def ag_post(key, n, owner, cols, dz):
+        ref = gfc.at[c_rows(owner), cols]
+        post(key, [remote(ref, ref, ag_s.at[n], ag_r.at[n], dev(0, 0, 0, dz))])
 
     for cs in range(4):
         for d in range(2):
@@ -311,14 +322,10 @@
             for j in range(2):
                 value = value + slot(d, 4, j, cs)[...].astype(F32)
         gfc[c_rows(z), pl.ds(*SETS[cs])] = value.astype(BF16)
-
-    def ag_post(key, n, owner, cols, dz):
-        ref = gfc.at[c_rows(owner), cols]
-        post(key, [remote(ref, ref, ag_s.at[n], ag_r.at[n], dev(0, 0, 0, dz))])
-
-    for cs in range(2):
-        for d in range(2):
-            ag_post(("second", d, cs), d * 2 + cs, z, pl.ds(*ENDS[cs]), 2 if d == 0 else 6)
+        if cs % 2 == 1:
+            half = cs // 2
+            for d in range(2):
+                ag_post(("second", d, half), d * 2 + half, z, pl.ds(*ENDS[half]), 2 if d == 0 else 6)
     for d in range(2):
         ag_post(("next", d), 4 + d, z, pl.ds(0, 896), 1 if d == 0 else 7)
 
@@ -346,17 +353,18 @@
     lane = lax.broadcasted_iota(jnp.int32, (1, 64), 1)
     for s in range(64):
         ids = jnp.where(lane == s, qi[s], ids)
-    doc = lax.broadcasted_iota(jnp.int32, (16, 256), 0)
-    position = lax.broadcasted_iota(jnp.int32, (16, 256), 1)
-    first = jnp.zeros((16, 256), jnp.int32)
-    last = jnp.zeros((16, 256), jnp.int32)
+    lanes = lax.broadcasted_iota(jnp.int32, (1, 128), 1)
+    first = jnp.zeros((1, 128), jnp.int32)
+    last = jnp.zeros((1, 128), jnp.int32)
     start = jnp.int32(0)
     for n in range(16):
         stop = start + dl[n]
-        first = jnp.where(doc == n, start, first)
-        last = jnp.where(doc == n, stop, last)
+        for q in range(Q):
+            first = jnp.where(lanes == q * 16 + n, start, first)
+            last = jnp.where(lanes == q * 16 + n, stop, last)
         start = stop
-    member = ((position >= first) & (position < last)).astype(F32)
+    position = lax.broadcasted_iota(jnp.int32, (256, 128), 0)
+    member = (position >= first) & (position < last)
 
     arrive("q gather")
     arrive("core 2")
@@ -388,24 +396,17 @@
         for cs in range(2):
             arrive(("third", d, cs))
 
-    columns = []
+    by_query = jnp.zeros((256, 128), F32)
     for q in range(Q):
         acc = jnp.zeros((256, 128), F32)
         for g in range(GROUPS):
             acc = acc + gfc[:, g * 128:(g + 1) * 128].astype(F32) * mm[g, :, q * 128:(q + 1) * 128]
-        columns.append(acc)
-    spread = jnp.dot(
-        member, jnp.concatenate(columns, axis=1), precision=lax.Precision.HIGHEST, preferred_element_type=F32
-    )
-    column = lax.broadcasted_iota(jnp.int32, (16, 128), 1) - Q * lax.broadcasted_iota(jnp.int32, (16, 128), 0)
-    scores = jnp.zeros((16, 128), F32)
-    for q in range(Q):
-        value = jnp.sum(spread[:, q * 128:(q + 1) * 128], axis=1, keepdims=True)
-        scores = jnp.where(column == q, value, scores)
-    fa[line] = jnp.sum(scores, axis=0, keepdims=True)
+        token_scores = jnp.sum(acc, axis=1, keepdims=True)
+        by_query = jnp.where((lanes >= q * 16) & (lanes < q * 16 + 16), token_scores, by_query)
+    fa[line] = jnp.sum(jnp.where(member, by_query, 0.0), axis=0, keepdims=True)
     early = dict(sends)
     sends.clear()
-    all_to("f line", fa, line, 2, line_peer)
+    all_to("f line", fa, line, 2, line_peer, True)
     late = dict(sends)
     sends.clear()
     sends.update(early)
@@ -413,15 +414,11 @@
     sends.update(late)
     arrive("f line")
     fb[chip] = jnp.sum(fa[...], axis=0)
-    all_to("f plane", fb, chip, 3, plane_peer)
+    all_to("f plane", fb, chip, 3, plane_peer, True)
     arrive("f plane")
-    whole = jnp.broadcast_to(jnp.sum(fb[...], axis=0), (16, 128))
-    place = lax.broadcasted_iota(jnp.int32, (16, Q), 1)
-    result = jnp.zeros((16, Q), F32)
+    scores = jnp.sum(fb[...], axis=0)
     for q in range(Q):
-        value = jnp.sum(jnp.where(column == q, whole, 0.0), axis=1, keepdims=True)
-        result = jnp.where(place == q, value, result)
-    out[...] = result
+        out[q:q + 1, :] = scores[:, q * 16:(q + 1) * 16]
     finish()
 
 
@@ -430,7 +427,7 @@
     vm = pltpu.VMEM
     return pl.pallas_call(
         kernel,
-        out_shape=jax.ShapeDtypeStruct((16, Q), F32),
+        out_shape=jax.ShapeDtypeStruct((Q, 16), F32),
         in_specs=[pl.BlockSpec(memory_space=pl.ANY)] * 7 + [pl.BlockSpec(memory_space=pltpu.SMEM)] * 2,
         out_specs=pl.BlockSpec(memory_space=pltpu.VMEM),
         scratch_shapes=[
@@ -455,7 +452,7 @@
         compiler_params=pltpu.CompilerParams(
             collective_id=0, has_side_effects=True, vmem_limit_bytes=63 << 20
         ),
-    )(*args)
+    )(*args).T
 
 
 def solution(mesh):

time: 58.6 us -> 57.7 us (0.985)
  Pallas kernels: 57.1 us -> 56.3 us
    pallas_call x1 -> x0, local copies, waits for them, and re-layouts: 1.35 us -> none  [local(): pl.pallas_call(kernel, out_shape=jax.ShapeDtypeStruct((16, Q), F32), in_s...]
    unnamed x0 -> x1, local copies, waits for them, and re-layouts: none -> 1.26 us
    pallas_call x1, Pallas kernels: 57.1 us -> 56.3 us  [local(): pl.pallas_call(kernel, out_shape=jax.ShapeDtypeStruct((Q, 16), F32), in_s...]
where the time goes in v5:
time: 57.7 us; the launch traced here: 57.6 us
  Pallas kernels  56.3 us (98%)
  local copies, waits for them, and re-layouts  1.26 us (2%)
    pallas_call x1, Pallas kernels, local(): pl.pallas_call(kernel, out_shape=jax.ShapeDtypeStruct((Q, 16), F32), in_s...  56.3 us
    unnamed x1, local copies, waits for them, and re-layouts  1.26 us

profile of v5, /device:TPU:1, one launch (start us, length us, event | category | flops | bytes accessed | tf_op | source)
XLA Modules:
  0.0 57.6 jit_solution(6281164521099912591)
XLA Ops:
  0.0 56.3 %influence.1 = f32[4,16]{1,0:T(4,128)} custom-call(bf16[256,1792]{1,0:T(8,128)(2,1)} %cg.1, bf16[256,256]{1,0:T(8,128)(2,1)} %ca.1, bf16[64,1792]{1,0:T(8,128)(2,1)} %qg.1, bf16[64,256]{1,0:T(8,128)(2,1)} %qa.1, bf16[1792,1792]{1,0:T(8,128)(2,1)} %eo.1, bf16[256,1024]{1,0:T(8,128)(2,1)} %ei.1, bf16[1792,1024]{1,0:T(8,128)(2,1)} %ev.1, s32[16]{0:T(128)} %dl.1, ...), custom_call_target="tpu_custom_call" | custom-call | tf_op jit(solution)/shard_map/influence/pallas_call | solution.py:428
  56.3 1.3 %copy.11 = f32[16,4]{0,1:T(4,128)} copy(f32[16,4]{0,1:T(4,128)} %bitcast.1) | data formatting | bytes 512

commit v6 on v5

--- a/solution.py
+++ b/solution.py
@@ -227,13 +227,13 @@
     for g in range(4):
         rotate(g)
     pl.semaphore_wait(barrier, 30)
+    other = pl.ds(pl.multiple_of((1 - c) * 512, 512), 512)
+    mine = pl.ds(pl.multiple_of(c * 512, 512), 512)
+    post("core 1", [remote(apk.at[:, :, other], rap, co_s.at[0], co_r.at[0], dev(0, 0, 1, 0))])
     for cs in range(2):
         rs_c(cs, 1, cs)
     for cs in range(2):
         rs_c(1 - cs, 2, cs)
-    other = pl.ds(pl.multiple_of((1 - c) * 512, 512), 512)
-    mine = pl.ds(pl.multiple_of(c * 512, 512), 512)
-    post("core 1", [remote(apk.at[:, :, other], rap, co_s.at[0], co_r.at[0], dev(0, 0, 1, 0))])
     for g in range(4, 7):
         rotate(g)
     rs_q(0, 1)
@@ -281,8 +281,6 @@
     eb[chip] = jnp.sum(ea[...], axis=0)
     all_to("e plane", eb, chip, 1, plane_peer)
 
-    rs_step(3)
-
     arrive("scatter")
     piece_cols = pl.ds(pl.multiple_of(c * 512 + y * 128, 128), 128)
     afa[x, :, piece_cols] = jnp.sum(rda[...], axis=0).astype(BF16)
@@ -292,6 +290,8 @@
         return [remote(ref, ref, pr_s.at[1], pr_r.at[1], plane_peer(r))]
 
     exchange("gather", a_gather, [sized(afa.at[pl.ds(0, 3), :, pl.ds(0, 640)], pr_s.at[1], pr_r.at[1])])
+
+    rs_step(3)
 
     arrive("own")
 

time: 57.7 us -> 58.1 us (level)
  no operation moved by 1% of the time
where the time goes in v6:
time: 58.1 us; the launch traced here: 58 us
  Pallas kernels  56.7 us (98%)
  local copies, waits for them, and re-layouts  1.26 us (2%)
    pallas_call x1, Pallas kernels, local(): pl.pallas_call(kernel, out_shape=jax.ShapeDtypeStruct((Q, 16), F32), in_s...  56.7 us
    unnamed x1, local copies, waits for them, and re-layouts  1.26 us

profile of v6, /device:TPU:1, one launch (start us, length us, event | category | flops | bytes accessed | tf_op | source)
XLA Modules:
  0.0 58.0 jit_solution(7550810792245431833)
XLA Ops:
  0.0 56.7 %influence.1 = f32[4,16]{1,0:T(4,128)} custom-call(bf16[256,1792]{1,0:T(8,128)(2,1)} %cg.1, bf16[256,256]{1,0:T(8,128)(2,1)} %ca.1, bf16[64,1792]{1,0:T(8,128)(2,1)} %qg.1, bf16[64,256]{1,0:T(8,128)(2,1)} %qa.1, bf16[1792,1792]{1,0:T(8,128)(2,1)} %eo.1, bf16[256,1024]{1,0:T(8,128)(2,1)} %ei.1, bf16[1792,1024]{1,0:T(8,128)(2,1)} %ev.1, s32[16]{0:T(128)} %dl.1, ...), custom_call_target="tpu_custom_call" | custom-call | tf_op jit(solution)/shard_map/influence/pallas_call | solution.py:428
  56.8 1.3 %copy.11 = f32[16,4]{0,1:T(4,128)} copy(f32[16,4]{0,1:T(4,128)} %bitcast.1) | data formatting | bytes 512
